TPU v7x, 32 devices: a whole 2x2x4 slice. The times are simulated.
32 devices in a mesh: gx: 2 (over y), gy: 8 (over z, core), gz: 2 (over x).
Axes of the slice: x: 2, y: 2, z: 4, core: 2. Of those that a mesh axis runs over, the one named last changes fastest.
Arguments:
- flow_vector_lowres: float32 [3, 4, 256, 256], P(None, 'gz', 'gy', 'gx'), may hold values from -3 to 3
- heat_anomaly_lowres: float32 [4, 256, 256], P('gz', 'gy', 'gx'), may hold values from -6 to 6
- salt_content_anomaly: float32 [8, 512, 512], P('gz', ('gx', 'gy')), may hold values from -6 to 6
Outputs:
- updated_velocity: float32 [3, 4, 256, 256], P(None, 'gz', 'gy', 'gx')
- temperature_new: float32 [4, 256, 256], P('gz', 'gy', 'gx')
- salinity_new: float32 [8, 512, 512], P('gz', ('gx', 'gy'))
All inputs are finite; a program needn't handle non-finite values.
Results may differ from a plain program's by a relative error of at most 0.00002.
Values sent between devices are 32-bit elements; how exact they have to be, the bound alone decides.
A program may use at most 128 MiB of HBM per device.

v0:
```python
import jax
import jax.numpy as jnp
from jax import lax
from jax.sharding import PartitionSpec as P

time_step = 0.1
viscosity = 0.2
heat_diffusion = 0.15
salt_diffusion = 0.05
expansion = 1.0
thermal_expansion_curve = 0.5
contraction = 0.8
even_weights = (-0.0390625, 0.2734375, 0.8203125, -0.0546875)
odd_weights = (-0.0546875, 0.8203125, 0.2734375, -0.0390625)


def with_halo(array, sides, width):
    for axis, dim in sides:
        size, length = (lax.axis_size(axis), array.shape[dim])
        up = [(i, (i + 1) % size) for i in range(size - 1)]
        down = [(j, i) for i, j in up]
        last = lax.slice_in_dim(array, length - width, length, axis=dim)
        first = lax.slice_in_dim(array, 0, width, axis=dim)
        before = lax.ppermute(last, axis, up)
        after = lax.ppermute(first, axis, down)
        array = jnp.concatenate([before, array, after], axis=dim)
    return array


def refine(padded, along_dim):
    length = padded.shape[along_dim] - 4
    even_part = even_weights[0] * lax.slice_in_dim(padded, 0, length, axis=along_dim)
    odd_part = odd_weights[0] * lax.slice_in_dim(padded, 1, length + 1, axis=along_dim)
    for offset in range(1, 4):
        even_part = even_part + even_weights[offset] * lax.slice_in_dim(
            padded, offset, offset + length, axis=along_dim
        )
        odd_part = odd_part + odd_weights[offset] * lax.slice_in_dim(
            padded, offset + 1, offset + 1 + length, axis=along_dim
        )
    target = list(even_part.shape)
    target[along_dim] = 2 * length
    return jnp.stack([even_part, odd_part], axis=along_dim + 1).reshape(target)


def window(padded, target, along_dim, offset):
    leading = padded.ndim - 3
    starts = [0] * leading + [1, 1, 1]
    starts[leading + along_dim] = offset
    limits = [start_at + extent for start_at, extent in zip(starts, target)]
    return lax.slice(padded, starts, limits)


def tendency(field, padded, speeds, spacing, diffusion):
    advection = jnp.zeros(field.shape, jnp.float32)
    neighbours = jnp.zeros(field.shape, jnp.float32)
    for along_dim in range(3):
        below_cells = window(padded, field.shape, along_dim, 0)
        above_cells = window(padded, field.shape, along_dim, 2)
        advect_speed = speeds[along_dim]
        advection = (
            advection
            + jnp.maximum(advect_speed, 0.0) * (field - below_cells)
            + jnp.minimum(advect_speed, 0.0) * (above_cells - field)
        )
        neighbours = neighbours + below_cells + above_cells
    return diffusion * (neighbours - 6.0 * field) / (spacing * spacing) - advection / spacing


def coarse_rates(prognostic_variables, padded, buoyancy):
    diffusion = jnp.array([viscosity, viscosity, viscosity, heat_diffusion], jnp.float32).reshape(
        4, 1, 1, 1
    )
    coarse_tendency_rate = tendency(
        prognostic_variables,
        padded,
        (prognostic_variables[0], prognostic_variables[1], prognostic_variables[2]),
        1.0,
        diffusion,
    )
    return jnp.concatenate(
        [coarse_tendency_rate[:1] + buoyancy[None], coarse_tendency_rate[1:]], axis=0
    )


def restrict(refined_field):
    level_count = refined_field.shape[0]
    row_count = refined_field.shape[1]
    col_count = refined_field.shape[2]
    grouped = refined_field.reshape(level_count // 2, 2, row_count // 2, 2, col_count // 2, 2)
    return 0.125 * jnp.sum(grouped, axis=(1, 3, 5))


def fine_rates(refined, salt_content_anomaly, salt_padded):
    salt_rate = tendency(
        salt_content_anomaly, salt_padded, (refined[0], refined[2], refined[1]), 0.5, salt_diffusion
    )
    buoyant = (
        expansion * refined[3] * (1.0 + thermal_expansion_curve * refined[3])
        - contraction * salt_content_anomaly
    )
    return (salt_rate, restrict(buoyant))


def heun_rates(prognostic_variables, salt_content_anomaly):
    salt_rim = with_halo(salt_content_anomaly, ((("gx", "gy"), 1), ("gz", 0)), 1)
    salt_padded = jnp.pad(salt_rim, ((0, 0), (0, 0), (1, 1)))
    pencil = lax.all_to_all(
        jnp.transpose(prognostic_variables, (0, 1, 3, 2)),
        "gy",
        split_axis=2,
        concat_axis=3,
        tiled=True,
    )
    grown_rim = with_halo(pencil, ((("gx", "gy"), 2), ("gz", 1)), 2)
    grown_rim = jnp.pad(grown_rim, ((0, 0), (0, 0), (0, 0), (2, 2)))
    refined = refine(refine(refine(grown_rim, 1), 2), 3)
    near_rim = with_halo(prognostic_variables, (("gx", 3), ("gy", 2), ("gz", 1)), 1)
    salt_rate, column_pencil_buoyancy = fine_rates(refined, salt_content_anomaly, salt_padded)
    tile_buoyancy = lax.all_to_all(
        column_pencil_buoyancy, "gy", split_axis=2, concat_axis=1, tiled=True
    )
    return (
        coarse_rates(prognostic_variables, near_rim, jnp.transpose(tile_buoyancy, (0, 2, 1))),
        salt_rate,
    )


def on_device(flow_vector_lowres, heat_anomaly_lowres, salt_content_anomaly):
    prognostic_variables = jnp.concatenate([flow_vector_lowres, heat_anomaly_lowres[None]], axis=0)
    coarse_tendency_rate, salt_rate = heun_rates(prognostic_variables, salt_content_anomaly)
    fields_mid = prognostic_variables + time_step * coarse_tendency_rate
    salt_mid = salt_content_anomaly + time_step * salt_rate
    coarse_rate_mid, salt_rate_mid = heun_rates(fields_mid, salt_mid)
    fields_end = 0.5 * prognostic_variables + 0.5 * (fields_mid + time_step * coarse_rate_mid)
    salt_end = 0.5 * salt_content_anomaly + 0.5 * (salt_mid + time_step * salt_rate_mid)
    return (fields_end[:3], fields_end[3], salt_end)


def solution(mesh):
    in_specs = (P(None, "gz", "gy", "gx"), P("gz", "gy", "gx"), P("gz", ("gx", "gy"), None))
    out_specs = (P(None, "gz", "gy", "gx"), P("gz", "gy", "gx"), P("gz", ("gx", "gy"), None))
    return jax.shard_map(
        on_device, mesh=mesh, in_specs=in_specs, out_specs=out_specs, check_vma=False
    )
```

profile of v0, /device:TPU:0, one launch (start us, length us, event | category | flops | bytes accessed | tf_op | source)
XLA Modules:
  0.0 224.3 jit_solution(3786498590382253645)
XLA Ops:
  3.2 6.3 %all-to-all-start = ((f32[8,1,4096]{2,1,0:T(1,128)}), f32[8,1,4096]{2,1,0:T(1,128)S(1)}, u32[]{:S(2)}, u32[]{:S(2)}) async-start(f32[8,1,4096]{2,1,0:T(1,128)} %reshape.76), calls=%async_computation | async-start | bytes 262144 | tf_op jit(solution)/shard_map/all_to_all | solution.py:108
  10.5 3.4 %collective-permute-start = (f32[4,2,32,1]{3,2,1,0:T(8,128)S(1)}, f32[4,2,32,1]{3,2,1,0:T(8,128)S(1)}, u32[]{:S(2)}, u32[]{:S(2)}) collective-permute-start(f32[4,2,32,1]{3,2,1,0:T(8,128)S(1)} %get-tuple-element.91), channel_id=1, source_target_pairs={{0,16},{1,17},{2,18},{3,19},{4,20},{5,21},{6,22},{7,23},{8,24},{9,... | collective-permute-start | bytes 3080 | tf_op jit(solution)/shard_map/ppermute | solution.py:24
  22.4 2.6 %collective-permute-start.2 = (f32[4,2,1,130]{3,0,2,1:T(4,128)S(1)}, f32[4,2,1,130]{3,0,2,1:T(4,128)S(1)}, u32[]{:S(2)}, u32[]{:S(2)}) collective-permute-start(f32[4,2,1,130]{3,0,2,1:T(4,128)S(1)} %copy.592), channel_id=1, source_target_pairs={{0,2},{2,4},{4,6},{6,8},{8,10},{10,12},{12,14},{1,3},{3,5},{5,7},{... | collective-permute-start | bytes 12488 | tf_op jit(solution)/shard_map/ppermute | solution.py:24
  30.5 3.5 %collective-permute-start.4 = (f32[4,1,34,130]{3,2,1,0:T(8,128)S(1)}, f32[4,1,34,130]{3,2,1,0:T(8,128)S(1)}, u32[]{:S(2)}, u32[]{:S(2)}) collective-permute-start(f32[4,1,34,130]{3,2,1,0:T(8,128)S(1)} %get-tuple-element.70), channel_id=1, source_target_pairs={{0,1},{2,3},{4,5},{6,7},{8,9},{10,11},{12,13},{14,15},{16,17},{18,... | collective-permute-start | bytes 212168 | tf_op jit(solution)/shard_map/ppermute | solution.py:24
  37.9 4.0 %collective-permute-start.6 = (f32[4,2,2,256]{3,2,1,0:T(2,128)S(1)}, f32[4,2,2,256]{3,2,1,0:T(2,128)S(1)}, u32[]{:S(2)}, u32[]{:S(2)}) collective-permute-start(f32[4,2,2,256]{3,2,1,0:T(2,128)S(1)} %get-tuple-element.89), channel_id=1, source_target_pairs={{0,2},{2,4},{4,6},{6,8},{8,10},{10,12},{12,14},{14,16},{16,18},{18... | collective-permute-start | bytes 49160 | tf_op jit(solution)/shard_map/ppermute | solution.py:24
  44.1 4.3 %collective-permute-start.22 = (f32[1,34,512]{2,1,0:T(8,128)S(1)}, f32[1,34,512]{2,1,0:T(8,128)S(1)}, u32[]{:S(2)}, u32[]{:S(2)}) collective-permute-start(f32[1,34,512]{2,1,0:T(8,128)S(1)} %get-tuple-element.73), channel_id=1, source_target_pairs={{0,1},{2,3},{4,5},{6,7},{8,9},{10,11},{12,13},{14,15},{16,17},{18,... | collective-permute-start | bytes 208904 | tf_op jit(solution)/shard_map/ppermute | solution.py:24
  49.8 4.6 %collective-permute-start.8 = (f32[4,2,20,256]{3,2,1,0:T(8,128)S(1)}, f32[4,2,20,256]{3,2,1,0:T(8,128)S(1)}, u32[]{:S(2)}, u32[]{:S(2)}) collective-permute-start(f32[4,2,20,256]{3,2,1,0:T(8,128)S(1)} %pad_maximum_fusion.25), channel_id=1, source_target_pairs={{0,1},{2,3},{4,5},{6,7},{8,9},{10,11},{12,13},{14,15},{16,17},{18,... | collective-permute-start | bytes 491528 | tf_op jit(solution)/shard_map/ppermute | solution.py:24
  59.6 3.9 %collective-permute-done.9 = f32[4,2,20,256]{3,2,1,0:T(8,128)S(1)} collective-permute-done((f32[4,2,20,256]{3,2,1,0:T(8,128)S(1)}, f32[4,2,20,256]{3,2,1,0:T(8,128)S(1)}, u32[]{:S(2)}, u32[]{:S(2)}) %collective-permute-start.9) | collective-permute-done | bytes 163872 | tf_op jit(solution)/shard_map/ppermute | solution.py:25
  68.7 18.1 %reshape.72 = f32[2,2,16,2,256,2]{5,4,3,2,1,0:T(8,128)} reshape(f32[4,32,512]{2,1,0:T(8,128)S(1)} %multiply_subtract_fusion.1) | data formatting | bytes 524288 | tf_op jit(solution)/shard_map/reshape | solution.py:90
  86.8 7.0 %reduce_sum.18 = f32[2,16,256]{2,1,0:T(8,128)S(1)} reduce(f32[2,2,16,2,256,2]{5,4,3,2,1,0:T(8,128)} %reshape.72, f32[]{:T(128)} %constant.15.clone.1), dimensions={1,3,5}, to_apply=%region_0.1 | reduce | flops 57344 | bytes 294916 | tf_op jit(solution)/shard_map/reduce_sum | solution.py:91
  94.9 5.3 %all-to-all-start.1 = ((f32[8,1,1024]{2,1,0:T(1,128)}), f32[8,1,1024]{2,1,0:T(1,128)S(1)}, u32[]{:S(2)}, u32[]{:S(2)}) async-start(f32[8,1,1024]{2,1,0:T(1,128)} %reshape.78), calls=%async_computation.1 | async-start | bytes 65536 | tf_op jit(solution)/shard_map/all_to_all | solution.py:120
  102.5 3.5 %all-to-all-done.1 = f32[8,1,1024]{2,1,0:T(1,128)S(1)} async-done(((f32[8,1,1024]{2,1,0:T(1,128)}), f32[8,1,1024]{2,1,0:T(1,128)S(1)}, u32[]{:S(2)}, u32[]{:S(2)}) %all-to-all-start.1) | async-done | bytes 32800 | tf_op jit(solution)/shard_map/all_to_all | solution.py:120
  109.8 4.7 %collective-permute-start.10 = (f32[4,2,32,1]{3,2,1,0:T(8,128)}, f32[4,2,32,1]{3,2,1,0:T(8,128)S(1)}, u32[]{:S(2)}, u32[]{:S(2)}) collective-permute-start(f32[4,2,32,1]{3,2,1,0:T(8,128)} %get-tuple-element.87), channel_id=1, source_target_pairs={{0,16},{1,17},{2,18},{3,19},{4,20},{5,21},{6,22},{7,23},{8,24},{9,... | collective-permute-start | bytes 3080 | tf_op jit(solution)/shard_map/ppermute | solution.py:24
  123.3 3.4 %all-to-all-start.2 = ((f32[8,1,4096]{2,1,0:T(1,128)}), f32[8,1,4096]{2,1,0:T(1,128)S(1)}, u32[]{:S(2)}, u32[]{:S(2)}) async-start(f32[8,1,4096]{2,1,0:T(1,128)} %reshape.80), calls=%async_computation.2 | async-start | bytes 262144 | tf_op jit(solution)/shard_map/all_to_all | solution.py:108
  126.9 2.3 %collective-permute-start.12 = (f32[4,2,1,130]{3,0,2,1:T(4,128)S(1)}, f32[4,2,1,130]{3,0,2,1:T(4,128)S(1)}, u32[]{:S(2)}, u32[]{:S(2)}) collective-permute-start(f32[4,2,1,130]{3,0,2,1:T(4,128)S(1)} %copy.522), channel_id=1, source_target_pairs={{0,2},{2,4},{4,6},{6,8},{8,10},{10,12},{12,14},{1,3},{3,5},{5,7},{... | collective-permute-start | bytes 12488 | tf_op jit(solution)/shard_map/ppermute | solution.py:24
  131.1 2.2 collective-permute-done.13
  135.9 4.4 %collective-permute-start.16 = (f32[4,2,2,256]{3,2,1,0:T(2,128)S(1)}, f32[4,2,2,256]{3,2,1,0:T(2,128)S(1)}, u32[]{:S(2)}, u32[]{:S(2)}) collective-permute-start(f32[4,2,2,256]{3,2,1,0:T(2,128)S(1)} %get-tuple-element.79), channel_id=1, source_target_pairs={{0,2},{2,4},{4,6},{6,8},{8,10},{10,12},{12,14},{14,16},{16,18},{18... | collective-permute-start | bytes 49160 | tf_op jit(solution)/shard_map/ppermute | solution.py:24
  141.7 2.2 collective-permute-start.14
  145.3 4.6 %collective-permute-start.18 = (f32[4,2,20,256]{3,2,1,0:T(8,128)S(1)}, f32[4,2,20,256]{3,2,1,0:T(8,128)S(1)}, u32[]{:S(2)}, u32[]{:S(2)}) collective-permute-start(f32[4,2,20,256]{3,2,1,0:T(8,128)S(1)} %pad_maximum_fusion.26), channel_id=1, source_target_pairs={{0,1},{2,3},{4,5},{6,7},{8,9},{10,11},{12,13},{14,15},{16,17},{18,... | collective-permute-start | bytes 491528 | tf_op jit(solution)/shard_map/ppermute | solution.py:24
  154.7 4.1 %collective-permute-done.19 = f32[4,2,20,256]{3,2,1,0:T(8,128)S(1)} collective-permute-done((f32[4,2,20,256]{3,2,1,0:T(8,128)S(1)}, f32[4,2,20,256]{3,2,1,0:T(8,128)S(1)}, u32[]{:S(2)}, u32[]{:S(2)}) %collective-permute-start.19) | collective-permute-done | bytes 163872 | tf_op jit(solution)/shard_map/ppermute | solution.py:25
  171.3 18.1 %reshape.75 = f32[2,2,16,2,256,2]{5,4,3,2,1,0:T(8,128)} reshape(f32[4,32,512]{2,1,0:T(8,128)S(1)} %get-tuple-element.23) | data formatting | bytes 524288 | tf_op jit(solution)/shard_map/reshape | solution.py:90
  189.4 7.0 %reduce_sum.19 = f32[2,16,256]{2,1,0:T(8,128)S(1)} reduce(f32[2,2,16,2,256,2]{5,4,3,2,1,0:T(8,128)} %reshape.75, f32[]{:T(128)} %constant.15.clone.1), dimensions={1,3,5}, to_apply=%region_1.2 | reduce | flops 57344 | bytes 294916 | tf_op jit(solution)/shard_map/reduce_sum | solution.py:91
  203.6 9.3 %all-to-all-start.3 = ((f32[8,1,1024]{2,1,0:T(1,128)}), f32[8,1,1024]{2,1,0:T(1,128)S(1)}, u32[]{:S(2)}, u32[]{:S(2)}) async-start(f32[8,1,1024]{2,1,0:T(1,128)} %reshape.82), calls=%async_computation.3 | async-start | bytes 65536 | tf_op jit(solution)/shard_map/all_to_all | solution.py:120
  215.8 2.9 %all-to-all-done.3 = f32[8,1,1024]{2,1,0:T(1,128)S(1)} async-done(((f32[8,1,1024]{2,1,0:T(1,128)}), f32[8,1,1024]{2,1,0:T(1,128)S(1)}, u32[]{:S(2)}, u32[]{:S(2)}) %all-to-all-start.3) | async-done | bytes 32800 | tf_op jit(solution)/shard_map/all_to_all | solution.py:120
  (200 shorter events, 90.8 us)
Async XLA Ops:
  3.2 32.3 %all-to-all-start = ((f32[8,1,4096]{2,1,0:T(1,128)}), f32[8,1,4096]{2,1,0:T(1,128)S(1)}, u32[]{:S(2)}, u32[]{:S(2)}) async-start(f32[8,1,4096]{2,1,0:T(1,128)} %reshape.76), calls=%async_computation | async-start | bytes 262144 | tf_op jit(solution)/shard_map/all_to_all | solution.py:108
  10.5 9.1 %collective-permute-start = (f32[4,2,32,1]{3,2,1,0:T(8,128)S(1)}, f32[4,2,32,1]{3,2,1,0:T(8,128)S(1)}, u32[]{:S(2)}, u32[]{:S(2)}) collective-permute-start(f32[4,2,32,1]{3,2,1,0:T(8,128)S(1)} %get-tuple-element.91), channel_id=1, source_target_pairs={{0,16},{1,17},{2,18},{3,19},{4,20},{5,21},{6,22},{7,23},{8,24},{9,... | collective-permute-start | bytes 3080 | tf_op jit(solution)/shard_map/ppermute | solution.py:24
  16.2 19.2 %collective-permute-start.20 = (f32[4,1,512]{2,0,1:T(4,128)S(1)}, f32[4,1,512]{2,0,1:T(4,128)S(1)}, u32[]{:S(2)}, u32[]{:S(2)}) collective-permute-start(f32[4,1,512]{2,0,1:T(4,128)S(1)} %copy.604), channel_id=1, source_target_pairs={{0,2},{2,4},{4,6},{6,8},{8,10},{10,12},{12,14},{14,16},{16,18},{18... | collective-permute-start | bytes 24584 | tf_op jit(solution)/shard_map/ppermute | solution.py:24
  18.3 17.1 %collective-permute-start.21 = (f32[4,1,512]{2,0,1:T(4,128)S(1)}, f32[4,1,512]{2,0,1:T(4,128)S(1)}, u32[]{:S(2)}, u32[]{:S(2)}) collective-permute-start(f32[4,1,512]{2,0,1:T(4,128)S(1)} %copy.605), channel_id=1, source_target_pairs={{2,0},{4,2},{6,4},{8,6},{10,8},{12,10},{14,12},{16,14},{18,16},{20... | collective-permute-start | bytes 24584 | tf_op jit(solution)/shard_map/ppermute | solution.py:25
  30.5 23.8 %collective-permute-start.4 = (f32[4,1,34,130]{3,2,1,0:T(8,128)S(1)}, f32[4,1,34,130]{3,2,1,0:T(8,128)S(1)}, u32[]{:S(2)}, u32[]{:S(2)}) collective-permute-start(f32[4,1,34,130]{3,2,1,0:T(8,128)S(1)} %get-tuple-element.70), channel_id=1, source_target_pairs={{0,1},{2,3},{4,5},{6,7},{8,9},{10,11},{12,13},{14,15},{16,17},{18,... | collective-permute-start | bytes 212168 | tf_op jit(solution)/shard_map/ppermute | solution.py:24
  34.1 21.6 %collective-permute-start.5 = (f32[4,1,34,130]{3,2,1,0:T(8,128)S(1)}, f32[4,1,34,130]{3,2,1,0:T(8,128)S(1)}, u32[]{:S(2)}, u32[]{:S(2)}) collective-permute-start(f32[4,1,34,130]{3,2,1,0:T(8,128)S(1)} %get-tuple-element.69), channel_id=1, source_target_pairs={{1,0},{3,2},{5,4},{7,6},{9,8},{11,10},{13,12},{15,14},{17,16},{19,... | collective-permute-start | bytes 212168 | tf_op jit(solution)/shard_map/ppermute | solution.py:25
  37.9 10.5 %collective-permute-start.6 = (f32[4,2,2,256]{3,2,1,0:T(2,128)S(1)}, f32[4,2,2,256]{3,2,1,0:T(2,128)S(1)}, u32[]{:S(2)}, u32[]{:S(2)}) collective-permute-start(f32[4,2,2,256]{3,2,1,0:T(2,128)S(1)} %get-tuple-element.89), channel_id=1, source_target_pairs={{0,2},{2,4},{4,6},{6,8},{8,10},{10,12},{12,14},{14,16},{16,18},{18... | collective-permute-start | bytes 49160 | tf_op jit(solution)/shard_map/ppermute | solution.py:24
  44.1 14.1 %collective-permute-start.22 = (f32[1,34,512]{2,1,0:T(8,128)S(1)}, f32[1,34,512]{2,1,0:T(8,128)S(1)}, u32[]{:S(2)}, u32[]{:S(2)}) collective-permute-start(f32[1,34,512]{2,1,0:T(8,128)S(1)} %get-tuple-element.73), channel_id=1, source_target_pairs={{0,1},{2,3},{4,5},{6,7},{8,9},{10,11},{12,13},{14,15},{16,17},{18,... | collective-permute-start | bytes 208904 | tf_op jit(solution)/shard_map/ppermute | solution.py:24
  48.4 9.8 %collective-permute-start.23 = (f32[1,34,512]{2,1,0:T(8,128)S(1)}, f32[1,34,512]{2,1,0:T(8,128)S(1)}, u32[]{:S(2)}, u32[]{:S(2)}) collective-permute-start(f32[1,34,512]{2,1,0:T(8,128)S(1)} %get-tuple-element.74), channel_id=1, source_target_pairs={{1,0},{3,2},{5,4},{7,6},{9,8},{11,10},{13,12},{15,14},{17,16},{19,... | collective-permute-start | bytes 208904 | tf_op jit(solution)/shard_map/ppermute | solution.py:25
  49.8 9.8 %collective-permute-start.8 = (f32[4,2,20,256]{3,2,1,0:T(8,128)S(1)}, f32[4,2,20,256]{3,2,1,0:T(8,128)S(1)}, u32[]{:S(2)}, u32[]{:S(2)}) collective-permute-start(f32[4,2,20,256]{3,2,1,0:T(8,128)S(1)} %pad_maximum_fusion.25), channel_id=1, source_target_pairs={{0,1},{2,3},{4,5},{6,7},{8,9},{10,11},{12,13},{14,15},{16,17},{18,... | collective-permute-start | bytes 491528 | tf_op jit(solution)/shard_map/ppermute | solution.py:24
  54.3 9.1 %collective-permute-start.9 = (f32[4,2,20,256]{3,2,1,0:T(8,128)S(1)}, f32[4,2,20,256]{3,2,1,0:T(8,128)S(1)}, u32[]{:S(2)}, u32[]{:S(2)}) collective-permute-start(f32[4,2,20,256]{3,2,1,0:T(8,128)S(1)} %pad_maximum_fusion.25), channel_id=1, source_target_pairs={{1,0},{3,2},{5,4},{7,6},{9,8},{11,10},{13,12},{15,14},{17,16},{19,... | collective-permute-start | bytes 491528 | tf_op jit(solution)/shard_map/ppermute | solution.py:25
  94.9 11.0 %all-to-all-start.1 = ((f32[8,1,1024]{2,1,0:T(1,128)}), f32[8,1,1024]{2,1,0:T(1,128)S(1)}, u32[]{:S(2)}, u32[]{:S(2)}) async-start(f32[8,1,1024]{2,1,0:T(1,128)} %reshape.78), calls=%async_computation.1 | async-start | bytes 65536 | tf_op jit(solution)/shard_map/all_to_all | solution.py:120
  109.8 16.9 %collective-permute-start.10 = (f32[4,2,32,1]{3,2,1,0:T(8,128)}, f32[4,2,32,1]{3,2,1,0:T(8,128)S(1)}, u32[]{:S(2)}, u32[]{:S(2)}) collective-permute-start(f32[4,2,32,1]{3,2,1,0:T(8,128)} %get-tuple-element.87), channel_id=1, source_target_pairs={{0,16},{1,17},{2,18},{3,19},{4,20},{5,21},{6,22},{7,23},{8,24},{9,... | collective-permute-start | bytes 3080 | tf_op jit(solution)/shard_map/ppermute | solution.py:24
  114.4 12.3 %collective-permute-start.11 = (f32[4,2,32,1]{3,2,1,0:T(8,128)}, f32[4,2,32,1]{3,2,1,0:T(8,128)S(1)}, u32[]{:S(2)}, u32[]{:S(2)}) collective-permute-start(f32[4,2,32,1]{3,2,1,0:T(8,128)} %get-tuple-element.88), channel_id=1, source_target_pairs={{16,0},{17,1},{18,2},{19,3},{20,4},{21,5},{22,6},{23,7},{24,8},{25... | collective-permute-start | bytes 3080 | tf_op jit(solution)/shard_map/ppermute | solution.py:25
  123.3 10.7 %all-to-all-start.2 = ((f32[8,1,4096]{2,1,0:T(1,128)}), f32[8,1,4096]{2,1,0:T(1,128)S(1)}, u32[]{:S(2)}, u32[]{:S(2)}) async-start(f32[8,1,4096]{2,1,0:T(1,128)} %reshape.80), calls=%async_computation.2 | async-start | bytes 262144 | tf_op jit(solution)/shard_map/all_to_all | solution.py:108
  135.9 9.3 %collective-permute-start.16 = (f32[4,2,2,256]{3,2,1,0:T(2,128)S(1)}, f32[4,2,2,256]{3,2,1,0:T(2,128)S(1)}, u32[]{:S(2)}, u32[]{:S(2)}) collective-permute-start(f32[4,2,2,256]{3,2,1,0:T(2,128)S(1)} %get-tuple-element.79), channel_id=1, source_target_pairs={{0,2},{2,4},{4,6},{6,8},{8,10},{10,12},{12,14},{14,16},{16,18},{18... | collective-permute-start | bytes 49160 | tf_op jit(solution)/shard_map/ppermute | solution.py:24
  141.7 9.5 %collective-permute-start.14 = (f32[4,1,34,130]{3,2,1,0:T(8,128)S(1)}, f32[4,1,34,130]{3,2,1,0:T(8,128)S(1)}, u32[]{:S(2)}, u32[]{:S(2)}) collective-permute-start(f32[4,1,34,130]{3,2,1,0:T(8,128)S(1)} %get-tuple-element.68), channel_id=1, source_target_pairs={{0,1},{2,3},{4,5},{6,7},{8,9},{10,11},{12,13},{14,15},{16,17},{18,... | collective-permute-start | bytes 212168 | tf_op jit(solution)/shard_map/ppermute | solution.py:24
  143.9 8.8 %collective-permute-start.15 = (f32[4,1,34,130]{3,2,1,0:T(8,128)S(1)}, f32[4,1,34,130]{3,2,1,0:T(8,128)S(1)}, u32[]{:S(2)}, u32[]{:S(2)}) collective-permute-start(f32[4,1,34,130]{3,2,1,0:T(8,128)S(1)} %get-tuple-element.67), channel_id=1, source_target_pairs={{1,0},{3,2},{5,4},{7,6},{9,8},{11,10},{13,12},{15,14},{17,16},{19,... | collective-permute-start | bytes 212168 | tf_op jit(solution)/shard_map/ppermute | solution.py:25
  145.3 9.4 %collective-permute-start.18 = (f32[4,2,20,256]{3,2,1,0:T(8,128)S(1)}, f32[4,2,20,256]{3,2,1,0:T(8,128)S(1)}, u32[]{:S(2)}, u32[]{:S(2)}) collective-permute-start(f32[4,2,20,256]{3,2,1,0:T(8,128)S(1)} %pad_maximum_fusion.26), channel_id=1, source_target_pairs={{0,1},{2,3},{4,5},{6,7},{8,9},{10,11},{12,13},{14,15},{16,17},{18,... | collective-permute-start | bytes 491528 | tf_op jit(solution)/shard_map/ppermute | solution.py:24
  149.8 9.0 %collective-permute-start.19 = (f32[4,2,20,256]{3,2,1,0:T(8,128)S(1)}, f32[4,2,20,256]{3,2,1,0:T(8,128)S(1)}, u32[]{:S(2)}, u32[]{:S(2)}) collective-permute-start(f32[4,2,20,256]{3,2,1,0:T(8,128)S(1)} %pad_maximum_fusion.26), channel_id=1, source_target_pairs={{1,0},{3,2},{5,4},{7,6},{9,8},{11,10},{13,12},{15,14},{17,16},{19,... | collective-permute-start | bytes 491528 | tf_op jit(solution)/shard_map/ppermute | solution.py:25
  167.4 45.5 %collective-permute-start.24 = (f32[4,1,512]{2,0,1:T(4,128)S(1)}, f32[4,1,512]{2,0,1:T(4,128)S(1)}, u32[]{:S(2)}, u32[]{:S(2)}) collective-permute-start(f32[4,1,512]{2,0,1:T(4,128)S(1)} %copy.570), channel_id=1, source_target_pairs={{0,2},{2,4},{4,6},{6,8},{8,10},{10,12},{12,14},{14,16},{16,18},{18... | collective-permute-start | bytes 24584 | tf_op jit(solution)/shard_map/ppermute | solution.py:24
  168.8 44.1 %collective-permute-start.25 = (f32[4,1,512]{2,0,1:T(4,128)S(1)}, f32[4,1,512]{2,0,1:T(4,128)S(1)}, u32[]{:S(2)}, u32[]{:S(2)}) collective-permute-start(f32[4,1,512]{2,0,1:T(4,128)S(1)} %copy.571), channel_id=1, source_target_pairs={{2,0},{4,2},{6,4},{8,6},{10,8},{12,10},{14,12},{16,14},{18,16},{20... | collective-permute-start | bytes 24584 | tf_op jit(solution)/shard_map/ppermute | solution.py:25
  203.6 15.0 %all-to-all-start.3 = ((f32[8,1,1024]{2,1,0:T(1,128)}), f32[8,1,1024]{2,1,0:T(1,128)S(1)}, u32[]{:S(2)}, u32[]{:S(2)}) async-start(f32[8,1,1024]{2,1,0:T(1,128)} %reshape.82), calls=%async_computation.3 | async-start | bytes 65536 | tf_op jit(solution)/shard_map/all_to_all | solution.py:120
  213.0 9.9 %collective-permute-start.26 = (f32[1,34,512]{2,1,0:T(8,128)S(1)}, f32[1,34,512]{2,1,0:T(8,128)S(1)}, u32[]{:S(2)}, u32[]{:S(2)}) collective-permute-start(f32[1,34,512]{2,1,0:T(8,128)S(1)} %get-tuple-element.71), channel_id=1, source_target_pairs={{0,1},{2,3},{4,5},{6,7},{8,9},{10,11},{12,13},{14,15},{16,17},{18,... | collective-permute-start | bytes 208904 | tf_op jit(solution)/shard_map/ppermute | solution.py:24
  (21 other events, 250.4 us)
where the time goes:
time: 227 us; the launch traced here: 224 us
  starting transfers between devices  88.2 us (39%)
  local copies, waits for them, and re-layouts  71 us (31%)
  other arithmetic  41 us (18%)
  waiting for transfers between devices  22.4 us (10%)
    ppermute x14, starting transfers between devices, with_halo(): before = lax.ppermute(last, axis, up)  45.6 us
    reshape x2, local copies, waits for them, and re-layouts, restrict(): refined_field.reshape(level_count // 2, 2, row_count // 2, 2, col_count /...  36.2 us
    ppermute x14, starting transfers between devices, with_halo(): after = lax.ppermute(first, axis, down)  18.3 us
    ppermute x14, waiting for transfers between devices, with_halo(): after = lax.ppermute(first, axis, down)  15.9 us
    all_to_all x2, starting transfers between devices, heun_rates(): lax.all_to_all(column_pencil_buoyancy, 'gy', split_axis=2, concat_axis=1,...  14.6 us
    reduce_sum x2, other arithmetic, restrict(): return 0.125 * jnp.sum(grouped, axis=(1, 3, 5))  14.1 us
    all_to_all x2, starting transfers between devices, heun_rates(): lax.all_to_all(jnp.transpose(prognostic_variables, (0, 1, 3, 2)), 'gy', s...  9.7 us
    max x12, local copies, waits for them, and re-layouts, tendency(): jnp.maximum(advect_speed, 0.0) * (field - below_cells)  7.5 us
  transfers between devices with their start and end apart: 32, of which 9 were waited for; matrix products, arithmetic and copies ran while one was open for 28% of the time, Pallas kernels for 0%

commit v1 on v0

v1 whole, which is shorter than its diff:
```python
import functools

import jax
import jax.numpy as jnp
from jax import lax
from jax.experimental import pallas as pl
from jax.experimental.pallas import tpu as pltpu
from jax.sharding import PartitionSpec as P

time_step = 0.1
viscosity = 0.2
heat_diffusion = 0.15
salt_diffusion = 0.05
expansion = 1.0
thermal_expansion_curve = 0.5
contraction = 0.8
even_weights = (-0.0390625, 0.2734375, 0.8203125, -0.0546875)
odd_weights = (-0.0546875, 0.8203125, 0.2734375, -0.0390625)
diffusion = (viscosity, viscosity, viscosity, heat_diffusion)
OFF = 8
WIDE = 4


def split_dot(value, matrix, dims):
    rows = value.shape[0]
    high = value.astype(jnp.bfloat16)
    rest = value - high.astype(jnp.float32)
    middle = rest.astype(jnp.bfloat16)
    low = (rest - middle.astype(jnp.float32)).astype(jnp.bfloat16)
    stacked = jnp.concatenate([high, middle, low], axis=0)
    out = lax.dot_general(stacked, matrix, (dims, ((), ())), preferred_element_type=jnp.float32)
    return out[:rows] + (out[rows : 2 * rows] + out[2 * rows :])


def taps(weights, values):
    total = weights[0] * values[0]
    for weight, value in zip(weights[1:], values[1:]):
        total = total + weight * value
    return total


def advect(speed, centre, below, above):
    return jnp.maximum(speed, 0.0) * (centre - below) + jnp.minimum(speed, 0.0) * (above - centre)


def kernel(
    ngx, n, nr, nc, cx, ny,
    flow, heat, salt, vel_out, heat_out, salt_out,
    turned, message, edge, got, got_edge, fields, mids, cols, cols_mid, warm, fine,
    grains, grains_mid, mean_salt, buoy, outgoing, landed, fold, widen,
    main_send, main_recv, pass_send, edge_send, edge_recv, mean_send, mean_recv,
    rim_send, rim_recv, end_send, end_recv,
):
    gx, gy, gz = lax.axis_index("gx"), lax.axis_index("gy"), lax.axis_index("gz")
    other = 1 - gz
    r = gx * n + gy
    last = ngx * n - 1
    frame = nr + 2 * WIDE
    padded = nr + 2 * OFF
    f32 = jnp.float32

    def at(x, y, z):
        return {"gx": x, "gy": y, "gz": z}

    up_x, up_y = jnp.where(gy == n - 1, gx + 1, gx), jnp.where(gy == n - 1, 0, gy + 1)
    dn_x, dn_y = jnp.where(gy == 0, gx - 1, gx), jnp.where(gy == 0, n - 1, gy - 1)

    barrier = pltpu.get_barrier_semaphore()

    def greet(x, y, z):
        pl.semaphore_signal(barrier, inc=1, device_id=at(x, y, z), device_id_type=pl.DeviceIdType.MESH)

    for d in range(1, n):
        greet(gx, lax.rem(gy + d, n), gz)
    greet(gx, gy, other)

    @pl.when(r > 0)
    def _():
        greet(dn_x, dn_y, gz)
        greet(dn_x, dn_y, other)

    @pl.when(r < last)
    def _():
        greet(up_x, up_y, gz)
        greet(up_x, up_y, other)

    takes_low = jnp.logical_and(gy == 0, gx > 0)
    takes_high = jnp.logical_and(gy == n - 1, gx < ngx - 1)

    @pl.when(takes_low)
    def _():
        for j in range(n):
            for z in range(2):
                greet(gx - 1, j, z)

    @pl.when(takes_high)
    def _():
        for j in range(n):
            for z in range(2):
                greet(gx + 1, j, z)

    tile = jnp.concatenate([flow[...].reshape(6 * cx, ny), heat[...].reshape(2 * cx, ny)], axis=0)
    lanes = 8 * cx
    zero8 = jnp.zeros((8, lanes), f32)
    turned[0:8] = zero8
    turned[8 + ny : 16 + ny] = zero8
    turned[8 : 8 + ny] = tile.T
    for j in range(n):
        base = 8 + nr * j
        message[j, 0:nr] = turned[base : base + nr]
        message[j, nr : nr + 4] = turned[base + nr : base + nr + 4]
        message[j, nr + 4 : nr + 8] = turned[base - 4 : base]
    edge[0, 0:4] = zero8[:4]
    edge[0, 4:8] = turned[4 + ny : 8 + ny]
    edge[1, 0:4] = turned[8:12]
    edge[1, 4:8] = zero8[:4]

    lowers = jnp.where(gx > 0, 2, 0)
    highers = jnp.where(gx < ngx - 1, 2, 0)
    sides = jnp.where(r > 0, 2, 0) + jnp.where(r < last, 2, 0)
    pl.semaphore_wait(barrier, n + sides + lowers + highers)

    def remote(src, dst, send, recv, x, y, z):
        return pltpu.make_async_remote_copy(
            src_ref=src, dst_ref=dst, send_sem=send, recv_sem=recv,
            device_id=at(x, y, z), device_id_type=pl.DeviceIdType.MESH,
        )

    main = []
    for d in range(1, n):
        to = lax.rem(gy + d, n)
        main.append(remote(message.at[to], got.at[gz, gy], main_send.at[d], main_recv.at[gz, gy], gx, to, gz))
        main[-1].start()

    def passed(j, z):
        return remote(got.at[z, j], got.at[z, j], pass_send.at[j], main_recv.at[z, j], gx, gy, other)

    got[gz, gy] = message[gy]
    passed(gy, gz).start()

    def edge_copy(which, z):
        x = gx + 1 if which == 0 else gx - 1
        y = 0 if which == 0 else n - 1
        return remote(edge.at[which], got_edge.at[gz, gy], edge_send.at[which, z], edge_recv.at[gz, gy], x, y, z)

    @pl.when(gx < ngx - 1)
    def _():
        for z in range(2):
            edge_copy(0, z).start()

    @pl.when(gx > 0)
    def _():
        for z in range(2):
            edge_copy(1, z).start()

    takes_edge = jnp.logical_or(takes_low, takes_high)

    @pl.when(jnp.logical_not(takes_edge))
    def _():
        got_edge[...] = jnp.zeros(got_edge.shape, f32)

    row_id = lax.broadcasted_iota(jnp.int32, (2 * nc, 2 * nc), 0)
    col_id = lax.broadcasted_iota(jnp.int32, (2 * nc, 2 * nc), 1)
    source = jnp.where(col_id < nc, 2 * col_id, 2 * (col_id - nc) + 1)
    fold[...] = jnp.where(row_id == source, 1.0, 0.0).astype(jnp.bfloat16)
    parts = []
    for lf in range(4):
        for rp in range(2):
            parts.append(
                jnp.concatenate(
                    [salt[lf, c, pl.ds(rp, nr, stride=2), :] for c in range(nc // 64)], axis=1
                )
            )
    folded = split_dot(jnp.concatenate(parts, axis=0), fold[...], ((1,), (0,)))
    for lf in range(4):
        for rp in range(2):
            k = (lf * 2 + rp) * nr
            grains[lf + 1, rp, OFF : OFF + nr] = folded[k : k + nr]

    def walls(buf):
        @pl.when(gz == 0)
        def _():
            buf[0] = jnp.zeros(buf.shape[1:], f32)

        @pl.when(gz == 1)
        def _():
            buf[5] = jnp.zeros(buf.shape[1:], f32)

        @pl.when(r == 0)
        def _():
            buf[1:5, 1, 0:OFF] = jnp.zeros((4, OFF, 2 * nc), f32)

        @pl.when(r == last)
        def _():
            buf[1:5, 0, OFF + nr : padded] = jnp.zeros((4, OFF, 2 * nc), f32)

    own = pl.ds(OFF, nr)

    def rims(buf, s):
        down = remote(
            buf.at[1:5, 0, OFF : OFF + 8], buf.at[1:5, 0, OFF + nr : padded],
            rim_send.at[s, 1], rim_recv.at[s, 1], dn_x, dn_y, gz,
        )
        up = remote(
            buf.at[1:5, 1, nr : OFF + nr], buf.at[1:5, 1, 0:OFF],
            rim_send.at[s, 2], rim_recv.at[s, 2], up_x, up_y, gz,
        )
        return down, up

    def rim_start(buf, s):
        down, up = rims(buf, s)
        level_copy(buf, s).start()

        @pl.when(r > 0)
        def _():
            down.start()

        @pl.when(r < last)
        def _():
            up.start()

    def level_copy(buf, s):
        return remote(
            buf.at[4 - 3 * gz, :, own], buf.at[5 * gz, :, own], rim_send.at[s, 0], rim_recv.at[s, 0], gx, gy, other
        )

    def level_landed(buf, s):
        return remote(
            buf.at[4 - 3 * gz, :, own], buf.at[5 * (1 - gz), :, own], rim_send.at[s, 0], rim_recv.at[s, 0], gx, gy, other
        )

    def rim_wait(buf, s):
        down, up = rims(buf, s)
        level_landed(buf, s).wait_recv()
        level_copy(buf, s).wait_send()

        @pl.when(r > 0)
        def _():
            up.wait_recv()
            down.wait_send()

        @pl.when(r < last)
        def _():
            down.wait_recv()
            up.wait_send()

    walls(grains)
    rim_start(grains, 0)

    def halves(value):
        return value[:, :nc] + value[:, nc:]

    for l in range(2):
        total = sum(grains[1 + 2 * l + p, q, OFF : OFF + nr] for p in range(2) for q in range(2))
        mean_salt[gz * 2 + l, OFF : OFF + nr] = 0.125 * halves(total)

    @pl.when(r == 0)
    def _():
        mean_salt[:, 0:OFF] = jnp.zeros((4, OFF, nc), f32)

    @pl.when(r == last)
    def _():
        mean_salt[:, OFF + nr : padded] = jnp.zeros((4, OFF, nc), f32)

    def mean_copy(k):
        mine = pl.ds(gz * 2, 2)
        if k == 0:
            part = mean_salt.at[mine, OFF : OFF + nr]
            return remote(part, part, mean_send.at[0], mean_recv.at[0], gx, gy, other)
        z = gz if k % 2 else other
        if k < 3:
            return remote(
                mean_salt.at[mine, nr : OFF + nr], mean_salt.at[mine, 0:OFF],
                mean_send.at[k], mean_recv.at[k], up_x, up_y, z,
            )
        return remote(
            mean_salt.at[mine, OFF : OFF + 8], mean_salt.at[mine, OFF + nr : padded],
            mean_send.at[k], mean_recv.at[k], dn_x, dn_y, z,
        )

    def mean_landed(k):
        from_z = gz if k % 2 else other
        theirs = pl.ds(from_z * 2, 2)
        if k == 0:
            part = mean_salt.at[theirs, OFF : OFF + nr]
        elif k < 3:
            part = mean_salt.at[theirs, 0:OFF]
        else:
            part = mean_salt.at[theirs, OFF + nr : padded]
        return remote(part, part, mean_send.at[k], mean_recv.at[k], gx, gy, other)

    mean_copy(0).start()

    @pl.when(r < last)
    def _():
        mean_copy(1).start()
        mean_copy(2).start()

    @pl.when(r > 0)
    def _():
        mean_copy(3).start()
        mean_copy(4).start()

    for d in range(1, n):
        j = lax.rem(gy + n - d, n)
        passed(j, gz).wait_recv()
        passed(j, gz).start()

    row_id = lax.broadcasted_iota(jnp.int32, (nc, 2 * nc), 0)
    col_id = lax.broadcasted_iota(jnp.int32, (nc, 2 * nc), 1)
    odd = col_id >= nc
    step = row_id - jnp.where(odd, col_id - nc - 1, col_id - 2)
    band = jnp.zeros((nc, 2 * nc), f32)
    for k in range(4):
        band = jnp.where(step == k, jnp.where(odd, odd_weights[k], even_weights[k]), band)
    widen[...] = band.astype(jnp.bfloat16)

    for buf in (cols, cols_mid):
        for f in range(4):
            for level in (0, 1, 6, 7):
                buf[f, level] = jnp.zeros((padded, 2 * nc), f32)
    for f in range(4):
        for level in (0, 5):
            fields[f, level] = jnp.zeros((padded, nc), f32)
            mids[f, level] = jnp.zeros((padded, nc), f32)

    @pl.when(takes_edge)
    def _():
        for z in range(2):
            for j in range(n):
                remote(edge.at[0], got_edge.at[z, j], edge_send.at[0, 0], edge_recv.at[z, j], gx, gy, other).wait_recv()

    chunk = lax.broadcasted_iota(jnp.int32, (nr + 8, 128), 1) // cx
    per = 128 // cx

    def gather_chunks(values, k):
        out = None
        for j, value in enumerate(values):
            shift = (cx * (j - k)) % 128
            moved = pltpu.roll(value, shift, axis=1) if shift else value
            out = moved if out is None else jnp.where(chunk[: value.shape[0]] == j, moved, out)
        return out

    def assemble(z):
        for t in range(lanes // 128):
            for a in range(n // per):
                values = []
                for j in range(per):
                    body = got[z, per * a + j, 0:nr, 128 * t : 128 * (t + 1)]
                    rim = (
                        got[z, per * a + j, nr : nr + 8, 128 * t : 128 * (t + 1)]
                        + got_edge[z, per * a + j, :, 128 * t : 128 * (t + 1)]
                    )
                    values.append(jnp.concatenate([body, rim], axis=0))
                for k in range(per):
                    pair = per * t + k
                    f, l = pair // 2, pair % 2
                    whole = gather_chunks(values, k)
                    where = slice(128 * a, 128 * (a + 1))
                    level = z * 2 + l + 1
                    fields[f, level, OFF : OFF + nr, where] = whole[:nr]
                    fields[f, level, 0:8, where] = whole[nr:]
                    fields[f, level, OFF + nr : padded, where] = whole[nr:]

    assemble(gz)
    for d in range(n):
        j = lax.rem(gy + d, n)
        passed(j, other).wait_recv()
    assemble(other)

    def widen_all(src, dst):
        for f in range(4):
            stack = src[f, 1:5].reshape(4 * padded, nc)
            wide = split_dot(stack, widen[...], ((1,), (0,)))
            for level in range(4):
                dst[f, level + 2] = wide[level * padded : (level + 1) * padded]

    widen_all(fields, cols)

    def level_taps(buf, f, base, lf):
        i, p = base + lf // 2, lf % 2
        return taps((even_weights, odd_weights)[p], [buf[f, i + k + p] for k in range(4)])

    def row_taps(read, start, count, rp):
        return taps((even_weights, odd_weights)[rp], [read(start - 2 + k + rp, count) for k in range(4)])

    def warm_mean(count, start, pick, l):
        total = None
        for lp in range(2):
            for rp in range(2):
                x = row_taps(lambda s, c: pick(2 * l + lp, s, c), start, count, rp)
                x = expansion * x * (1.0 + thermal_expansion_curve * x)
                total = x if total is None else total + x
        return 0.125 * halves(total)

    lo = OFF - WIDE

    for f in range(3):
        for lf in range(4):
            fine[f, lf] = level_taps(cols, f, 2 * gz, lf)

    rim_wait(grains, 0)
    lane = lax.broadcasted_iota(jnp.int32, (nr, nc), 1)

    def salt_rate(buf, lf, rp):
        centre = buf[lf + 1, rp, OFF : OFF + nr]
        lower, upper = buf[lf, rp, OFF : OFF + nr], buf[lf + 2, rp, OFF : OFF + nr]
        if rp == 0:
            before, after = buf[lf + 1, 1, OFF - 1 : OFF - 1 + nr], buf[lf + 1, 1, OFF : OFF + nr]
        else:
            before, after = buf[lf + 1, 0, OFF : OFF + nr], buf[lf + 1, 0, OFF + 1 : OFF + 1 + nr]
        even, uneven = centre[:, :nc], centre[:, nc:]
        left = jnp.concatenate([jnp.where(lane == 0, 0.0, pltpu.roll(uneven, 1, axis=1)), even], axis=1)
        right = jnp.concatenate([uneven, jnp.where(lane == nc - 1, 0.0, pltpu.roll(even, nc - 1, axis=1))], axis=1)
        w, u, v = [row_taps(lambda s, c: fine[f, lf, s : s + c], OFF, nr, rp) for f in range(3)]
        flux = advect(w, centre, lower, upper) + advect(v, centre, before, after) + advect(u, centre, left, right)
        around = (lower + upper) + (before + after) + (left + right)
        return centre, (4.0 * salt_diffusion) * (around - 6.0 * centre) - 2.0 * flux

    mean_mid = []
    for l in range(2):
        total = None
        for lf in (2 * l, 2 * l + 1):
            for rp in range(2):
                centre, rate = salt_rate(grains, lf, rp)
                mid = centre + time_step * rate
                grains_mid[lf + 1, rp, OFF : OFF + nr] = mid
                total = mid if total is None else total + mid
        mean_mid.append(0.125 * halves(total))
    walls(grains_mid)
    rim_start(grains_mid, 1)

    for lf in range(8):
        warm[lf] = level_taps(cols, 3, 0, lf)
    mean_landed(0).wait_recv()

    @pl.when(r > 0)
    def _():
        mean_landed(1).wait_recv()
        mean_landed(2).wait_recv()

    @pl.when(r < last)
    def _():
        mean_landed(3).wait_recv()
        mean_landed(4).wait_recv()

    for l in range(4):
        heat_part = warm_mean(frame, lo, lambda i, s, c: warm[i, s : s + c], l)
        buoy[l] = heat_part - contraction * mean_salt[l, lo : lo + frame]

    def coarse_step(buf, level, start, count, lift):
        here = lax.broadcasted_iota(jnp.int32, (count, nc), 1)
        rows = pl.ds(start, count)
        centres = [buf[f, level, rows] for f in range(4)]
        out = []
        for f in range(4):
            q = centres[f]
            lower, upper = buf[f, level - 1, rows], buf[f, level + 1, rows]
            before, after = buf[f, level, start - 1 : start - 1 + count], buf[f, level, start + 1 : start + 1 + count]
            left = jnp.where(here == 0, 0.0, pltpu.roll(q, 1, axis=1))
            right = jnp.where(here == nc - 1, 0.0, pltpu.roll(q, nc - 1, axis=1))
            flux = (
                advect(centres[0], q, lower, upper)
                + advect(centres[1], q, left, right)
                + advect(centres[2], q, before, after)
            )
            around = (lower + upper) + (before + after) + (left + right)
            rate = diffusion[f] * (around - 6.0 * q) - flux
            out.append((q, rate + lift if f == 0 else rate))
        return out

    row = lax.broadcasted_iota(jnp.int32, (frame, nc), 0) + (r * nr - WIDE)
    inside = jnp.logical_and(row >= 0, row < (last + 1) * nr)
    for f in range(4):
        for level in range(4):
            mids[f, level + 1, 0:8] = jnp.zeros((8, nc), f32)
            mids[f, level + 1, OFF + nr : padded] = jnp.zeros((8, nc), f32)
    for level in range(4):
        for f, (q, rate) in enumerate(coarse_step(fields, level + 1, lo, frame, buoy[level])):
            mids[f, level + 1, lo : lo + frame] = jnp.where(inside, q + time_step * rate, 0.0)

    widen_all(mids, cols_mid)
    for lf in range(4):
        warm[lf] = level_taps(cols_mid, 3, 2 * gz, lf)
    results = []
    for l in range(2):
        lift = warm_mean(nr, OFF, lambda i, s, c: warm[i, s : s + c], l) - contraction * mean_mid[l]
        level = gz * 2 + l + 1
        steps = coarse_step(mids, level, OFF, nr, lift)
        results.append(
            [0.5 * fields[f, level, OFF : OFF + nr] + 0.5 * (q + time_step * rate) for f, (q, rate) in enumerate(steps)]
        )
    for a in range(n // per):
        for t in range(lanes // 128):
            values = []
            for k in range(per):
                pair = per * t + k
                values.append(results[pair % 2][pair // 2][:, 128 * a : 128 * (a + 1)])
            for j in range(per):
                outgoing[per * a + j, :, 128 * t : 128 * (t + 1)] = gather_chunks(values, j)
    ends = []
    for d in range(1, n):
        to = lax.rem(gy + d, n)
        ends.append(remote(outgoing.at[to], landed.at[gy], end_send.at[d], end_recv.at[gy], gx, to, gz))
        ends[-1].start()
    landed[gy] = outgoing[gy]

    for f in range(3):
        for lf in range(4):
            fine[f, lf] = level_taps(cols_mid, f, 2 * gz, lf)
    rim_wait(grains_mid, 1)
    parts = []
    for lf in range(4):
        for rp in range(2):
            centre, rate = salt_rate(grains_mid, lf, rp)
            parts.append(0.5 * grains[lf + 1, rp, OFF : OFF + nr] + 0.5 * (centre + time_step * rate))
    whole = split_dot(jnp.concatenate(parts, axis=0), fold[...], ((1,), (1,)))
    for lf in range(4):
        for rp in range(2):
            k = (lf * 2 + rp) * nr
            for c in range(nc // 64):
                salt_out[lf, c, pl.ds(rp, nr, stride=2), :] = whole[k : k + nr, 128 * c : 128 * (c + 1)]

    for d in range(1, n):
        j = lax.rem(gy + n - d, n)
        remote(outgoing.at[j], landed.at[j], end_send.at[d], end_recv.at[j], gx, j, gz).wait_recv()
    back = landed[...].reshape(ny, lanes).T
    vel_out[...] = back[: 6 * cx].reshape(3, 2, cx, ny)
    heat_out[...] = back[6 * cx :].reshape(2, cx, ny)

    for copy in main + ends:
        copy.wait_send()
    for j in range(n):
        passed(j, gz).wait_send()
    mean_copy(0).wait_send()

    @pl.when(gx < ngx - 1)
    def _():
        for z in range(2):
            edge_copy(0, z).wait_send()

    @pl.when(gx > 0)
    def _():
        for z in range(2):
            edge_copy(1, z).wait_send()

    @pl.when(r < last)
    def _():
        mean_copy(1).wait_send()
        mean_copy(2).wait_send()

    @pl.when(r > 0)
    def _():
        mean_copy(3).wait_send()
        mean_copy(4).wait_send()


def on_device(ngx, n, flow, heat, salt):
    cx, ny = flow.shape[2], flow.shape[3]
    nr, nc = salt.shape[1] // 2, salt.shape[2] // 2
    padded = nr + 2 * OFF
    lanes = 8 * cx
    f32, dma = jnp.float32, pltpu.SemaphoreType.DMA
    vmem = pl.BlockSpec(memory_space=pltpu.VMEM)
    split = salt.reshape(4, 2 * nr, nc // 64, 128).transpose(0, 2, 1, 3)
    vel, temp, out = pl.pallas_call(
        functools.partial(kernel, ngx, n, nr, nc, cx, ny),
        out_shape=(
            jax.ShapeDtypeStruct(flow.shape, f32),
            jax.ShapeDtypeStruct(heat.shape, f32),
            jax.ShapeDtypeStruct(split.shape, f32),
        ),
        in_specs=[vmem] * 3,
        out_specs=(vmem,) * 3,
        scratch_shapes=[
            pltpu.VMEM((ny + 16, lanes), f32),
            pltpu.VMEM((n, nr + 8, lanes), f32),
            pltpu.VMEM((2, 8, lanes), f32),
            pltpu.VMEM((2, n, nr + 8, lanes), f32),
            pltpu.VMEM((2, n, 8, lanes), f32),
            pltpu.VMEM((4, 6, padded, nc), f32),
            pltpu.VMEM((4, 6, padded, nc), f32),
            pltpu.VMEM((4, 8, padded, 2 * nc), f32),
            pltpu.VMEM((4, 8, padded, 2 * nc), f32),
            pltpu.VMEM((8, padded, 2 * nc), f32),
            pltpu.VMEM((3, 4, padded, 2 * nc), f32),
            pltpu.VMEM((6, 2, padded, 2 * nc), f32),
            pltpu.VMEM((6, 2, padded, 2 * nc), f32),
            pltpu.VMEM((4, padded, nc), f32),
            pltpu.VMEM((4, nr + 2 * WIDE, nc), f32),
            pltpu.VMEM((n, nr, lanes), f32),
            pltpu.VMEM((n, nr, lanes), f32),
            pltpu.VMEM((2 * nc, 2 * nc), jnp.bfloat16),
            pltpu.VMEM((nc, 2 * nc), jnp.bfloat16),
            dma((n,)), dma((2, n)), dma((n,)), dma((2, 2)), dma((2, n)), dma((5,)), dma((5,)),
            dma((2, 3)), dma((2, 3)), dma((n,)), dma((n,)),
        ],
        compiler_params=pltpu.CompilerParams(
            collective_id=0, has_side_effects=True, vmem_limit_bytes=48 * 1024 * 1024
        ),
    )(flow, heat, split)
    return vel, temp, out.transpose(0, 2, 1, 3).reshape(salt.shape)


def solution(mesh):
    in_specs = (P(None, "gz", "gy", "gx"), P("gz", "gy", "gx"), P("gz", ("gx", "gy"), None))
    out_specs = (P(None, "gz", "gy", "gx"), P("gz", "gy", "gx"), P("gz", ("gx", "gy"), None))
    return jax.shard_map(
        functools.partial(on_device, mesh.shape["gx"], mesh.shape["gy"]),
        mesh=mesh, in_specs=in_specs, out_specs=out_specs, check_vma=False,
    )
```

time: 227 us -> 29.6 us (0.13); the launches traced: 224 us -> 29.5 us
  starting transfers between devices: 88.2 us -> 0 us
  local copies, waits for them, and re-layouts: 71 us -> 3.8 us
  other arithmetic: 41 us -> 0 us
  Pallas kernels: 0 us -> 25 us
  waiting for transfers between devices: 22.4 us -> 0 us
    ppermute x28 -> x0, starting transfers between devices: 63.9 us -> none  [the longest x14 45.6 us: with_halo(): before = lax.ppermute(last, axis, up)]
    reshape x2 -> x1, local copies, waits for them, and re-layouts: 36.2 us -> 0.73 us  [on_device(): return (vel, temp, out.transpose(0, 2, 1, 3).reshape(salt.shape))]
    pallas_call x0 -> x1, Pallas kernels: none -> 25 us  [on_device(): pl.pallas_call(functools.partial(kernel, ngx, n, nr, nc, cx, ny), out_sha...]
    all_to_all x4 -> x0, starting transfers between devices: 24.3 us -> none  [the longest x2 14.6 us: heun_rates(): lax.all_to_all(column_pencil_buoyancy, 'gy', split_axis=2, concat_axis=1,...]
    ppermute x28 -> x0, waiting for transfers between devices: 16 us -> none  [the longest x14 15.9 us: with_halo(): after = lax.ppermute(first, axis, down)]
    reduce_sum x2 -> x0, other arithmetic: 14.1 us -> none  [restrict(): return 0.125 * jnp.sum(grouped, axis=(1, 3, 5))]
    slice x18 -> x0, local copies, waits for them, and re-layouts: 7.98 us -> none  [the longest x2 2.3 us: refine(): lax.slice_in_dim(padded, offset + 1, offset + 1 + length, axis=along_dim)]
    max x12 -> x0, local copies, waits for them, and re-layouts: 7.5 us -> none  [tendency(): jnp.maximum(advect_speed, 0.0) * (field - below_cells)]
  transfers between devices with their start and end apart: 32 -> 0, of which waited for: 9 -> 0; matrix products, arithmetic and copies ran while one was open for 28% -> 0% of each run, Pallas kernels for 0% -> 0%
where the time goes in v1:
time: 29.6 us; the launch traced here: 29.5 us
  Pallas kernels  25 us (84%)
  local copies, waits for them, and re-layouts  3.8 us (13%)
  between operations  0.67 us (2%)
    pallas_call x1, Pallas kernels, on_device(): pl.pallas_call(functools.partial(kernel, ngx, n, nr, nc, cx, ny), out_sha...  25 us
    unnamed x8, local copies, waits for them, and re-layouts  3.05 us
    reshape x1, local copies, waits for them, and re-layouts, on_device(): return (vel, temp, out.transpose(0, 2, 1, 3).reshape(salt.shape))  0.73 us

profile of v1, /device:TPU:0, one launch (start us, length us, event | category | flops | bytes accessed | tf_op | source)
XLA Modules:
  0.0 29.5 jit_solution(14441111359657544852)
XLA Ops:
  0.6 0.0 copy-start
  0.6 0.0 copy-start.2
  0.7 0.9 %copy-done = f32[4,32,512]{2,1,0:T(8,128)S(1)} copy-done((f32[4,32,512]{2,1,0:T(8,128)S(1)}, f32[4,32,512]{2,1,0:T(8,128)}, u32[]{:S(2)}) %copy-start) | copy-done | bytes 262168
  1.6 0.0 copy-start.1
  1.6 0.0 copy-done.2
  1.6 0.9 %copy-done.1 = f32[3,2,32,128]{3,2,1,0:T(8,128)S(1)} copy-done((f32[3,2,32,128]{3,2,1,0:T(8,128)S(1)}, f32[3,2,32,128]{3,2,1,0:T(8,128)}, u32[]{:S(2)}) %copy-start.1) | copy-done | bytes 98328
  2.5 25.0 %shard_map.58 = (f32[3,2,32,128]{3,2,1,0:T(8,128)S(1)}, f32[2,32,128]{2,1,0:T(8,128)S(1)}, f32[4,4,32,128]{3,2,1,0:T(8,128)S(1)}) custom-call(f32[3,2,32,128]{3,2,1,0:T(8,128)S(1)} %copy-done.1, f32[2,32,128]{2,1,0:T(8,128)S(1)} %copy-done.2, f32[4,4,32,128]{3,2,1,0:T(8,128)S(1)} %bitcast_bitcast_fusion.salt), custom_call_target="tpu_custom_call" | custom-call | tf_op jit(solution)/shard_map/pallas_call | solution.py:566
  27.5 0.7 %copy_bitcast_fusion = f32[4,32,512]{2,1,0:T(8,128)} fusion(f32[4,4,32,128]{3,2,1,0:T(8,128)S(1)} %get-tuple-element.8), kind=kLoop, calls=%fused_computation | loop fusion | bytes 524288 | tf_op jit(solution)/shard_map/reshape | solution.py:602
  28.2 0.6 %copy.14 = f32[3,2,32,128]{3,2,1,0:T(8,128)} copy(f32[3,2,32,128]{3,2,1,0:T(8,128)S(1)} %get-tuple-element.12) | data formatting | bytes 196608
  28.8 0.6 %copy.15 = f32[2,32,128]{2,1,0:T(8,128)} copy(f32[2,32,128]{2,1,0:T(8,128)S(1)} %get-tuple-element.13) | data formatting | bytes 65536
  (1 shorter events, 0.0 us)
Async XLA Ops:
  0.6 1.0 %copy-start = (f32[4,32,512]{2,1,0:T(8,128)S(1)}, f32[4,32,512]{2,1,0:T(8,128)}, u32[]{:S(2)}) copy-start(f32[4,32,512]{2,1,0:T(8,128)} %param.5) | copy-start | bytes 786436
  0.6 1.0 %copy-start.2 = (f32[2,32,128]{2,1,0:T(8,128)S(1)}, f32[2,32,128]{2,1,0:T(8,128)}, u32[]{:S(2)}) copy-start(f32[2,32,128]{2,1,0:T(8,128)} %heat.1) | copy-start | bytes 98308
  1.6 0.9 %copy-start.1 = (f32[3,2,32,128]{3,2,1,0:T(8,128)S(1)}, f32[3,2,32,128]{3,2,1,0:T(8,128)}, u32[]{:S(2)}) copy-start(f32[3,2,32,128]{3,2,1,0:T(8,128)} %flow.1) | copy-start | bytes 294916

commit v2 on v1

--- a/solution.py
+++ b/solution.py
@@ -17,19 +17,24 @@
 even_weights = (-0.0390625, 0.2734375, 0.8203125, -0.0546875)
 odd_weights = (-0.0546875, 0.8203125, 0.2734375, -0.0390625)
 diffusion = (viscosity, viscosity, viscosity, heat_diffusion)
+VMEM = 64 * 1024 * 1024
 OFF = 8
 WIDE = 4
 
 
-def split_dot(value, matrix, dims):
+def split_dot(value, matrix, dims, count=3):
     rows = value.shape[0]
-    high = value.astype(jnp.bfloat16)
-    rest = value - high.astype(jnp.float32)
-    middle = rest.astype(jnp.bfloat16)
-    low = (rest - middle.astype(jnp.float32)).astype(jnp.bfloat16)
-    stacked = jnp.concatenate([high, middle, low], axis=0)
+    parts = []
+    for k in range(count):
+        parts.append(value.astype(jnp.bfloat16))
+        if k < count - 1:
+            value = value - parts[-1].astype(jnp.float32)
+    stacked = jnp.concatenate(parts, axis=0)
     out = lax.dot_general(stacked, matrix, (dims, ((), ())), preferred_element_type=jnp.float32)
-    return out[:rows] + (out[rows : 2 * rows] + out[2 * rows :])
+    total = out[(count - 1) * rows :]
+    for k in range(count - 2, -1, -1):
+        total = out[k * rows : (k + 1) * rows] + total
+    return total
 
 
 def taps(weights, values):
@@ -45,11 +50,11 @@
 
 def kernel(
     ngx, n, nr, nc, cx, ny,
-    flow, heat, salt, vel_out, heat_out, salt_out,
-    turned, message, edge, got, got_edge, fields, mids, cols, cols_mid, warm, fine,
+    flow_in, heat_in, salt_in, vel_out, heat_out, salt_out,
+    flow, heat, salt, turned, message, edge, got, got_edge, fields, mids, tall, fine,
     grains, grains_mid, mean_salt, buoy, outgoing, landed, fold, widen,
     main_send, main_recv, pass_send, edge_send, edge_recv, mean_send, mean_recv,
-    rim_send, rim_recv, end_send, end_recv,
+    rim_send, rim_recv, end_send, end_recv, load,
 ):
     gx, gy, gz = lax.axis_index("gx"), lax.axis_index("gy"), lax.axis_index("gz")
     other = 1 - gz
@@ -65,6 +70,14 @@
     up_x, up_y = jnp.where(gy == n - 1, gx + 1, gx), jnp.where(gy == n - 1, 0, gy + 1)
     dn_x, dn_y = jnp.where(gy == 0, gx - 1, gx), jnp.where(gy == 0, n - 1, gy - 1)
 
+    loads = [pltpu.make_async_copy(flow_in, flow, load.at[0]), pltpu.make_async_copy(heat_in, heat, load.at[1])]
+    for c in range(nc // 64):
+        loads.append(
+            pltpu.make_async_copy(salt_in.at[:, :, 128 * c : 128 * (c + 1)], salt.at[:, c], load.at[2 + c])
+        )
+    for copy in loads:
+        copy.start()
+
     barrier = pltpu.get_barrier_semaphore()
 
     def greet(x, y, z):
@@ -99,6 +112,8 @@
             for z in range(2):
                 greet(gx + 1, j, z)
 
+    loads[0].wait()
+    loads[1].wait()
     tile = jnp.concatenate([flow[...].reshape(6 * cx, ny), heat[...].reshape(2 * cx, ny)], axis=0)
     lanes = 8 * cx
     zero8 = jnp.zeros((8, lanes), f32)
@@ -163,6 +178,8 @@
     col_id = lax.broadcasted_iota(jnp.int32, (2 * nc, 2 * nc), 1)
     source = jnp.where(col_id < nc, 2 * col_id, 2 * (col_id - nc) + 1)
     fold[...] = jnp.where(row_id == source, 1.0, 0.0).astype(jnp.bfloat16)
+    for copy in loads[2:]:
+        copy.wait()
     parts = []
     for lf in range(4):
         for rp in range(2):
@@ -315,10 +332,9 @@
         band = jnp.where(step == k, jnp.where(odd, odd_weights[k], even_weights[k]), band)
     widen[...] = band.astype(jnp.bfloat16)
 
-    for buf in (cols, cols_mid):
-        for f in range(4):
-            for level in (0, 1, 6, 7):
-                buf[f, level] = jnp.zeros((padded, 2 * nc), f32)
+    for f in range(4):
+        for level in (0, 1, 6, 7):
+            tall[f, level] = jnp.zeros((2, frame, nc), f32)
     for f in range(4):
         for level in (0, 5):
             fields[f, level] = jnp.zeros((padded, nc), f32)
@@ -362,43 +378,59 @@
                     fields[f, level, 0:8, where] = whole[nr:]
                     fields[f, level, OFF + nr : padded, where] = whole[nr:]
 
+    lo = OFF - WIDE
+
+    def row_taps(buf, f, level, start, count, rp):
+        weights = (even_weights, odd_weights)[rp]
+        base = start - 2 + rp
+        return taps(weights, [buf[f, level, base + k : base + k + count] for k in range(4)])
+
+    def refine_rows(buf, z, start, count):
+        for l in range(2):
+            level = z * 2 + l
+            for rp in range(2):
+                for f in range(3):
+                    tall[f, level + 2, rp, 0:nr] = row_taps(buf, f, level + 1, OFF, nr, rp)
+                tall[3, level + 2, rp, 0:count] = row_taps(buf, 3, level + 1, start, count, rp)
+
     assemble(gz)
+    refine_rows(fields, gz, lo, frame)
     for d in range(n):
         j = lax.rem(gy + d, n)
         passed(j, other).wait_recv()
     assemble(other)
-
-    def widen_all(src, dst):
-        for f in range(4):
-            stack = src[f, 1:5].reshape(4 * padded, nc)
-            wide = split_dot(stack, widen[...], ((1,), (0,)))
-            for level in range(4):
-                dst[f, level + 2] = wide[level * padded : (level + 1) * padded]
-
-    widen_all(fields, cols)
-
-    def level_taps(buf, f, base, lf):
-        i, p = base + lf // 2, lf % 2
-        return taps((even_weights, odd_weights)[p], [buf[f, i + k + p] for k in range(4)])
-
-    def row_taps(read, start, count, rp):
-        return taps((even_weights, odd_weights)[rp], [read(start - 2 + k + rp, count) for k in range(4)])
-
-    def warm_mean(count, start, pick, l):
-        total = None
-        for lp in range(2):
-            for rp in range(2):
-                x = row_taps(lambda s, c: pick(2 * l + lp, s, c), start, count, rp)
-                x = expansion * x * (1.0 + thermal_expansion_curve * x)
-                total = x if total is None else total + x
-        return 0.125 * halves(total)
-
-    lo = OFF - WIDE
-
-    for f in range(3):
-        for lf in range(4):
-            fine[f, lf] = level_taps(cols, f, 2 * gz, lf)
-
+    refine_rows(fields, other, lo, frame)
+
+    def level_taps(f, base, lf, count):
+        p = lf % 2
+        values, weights = [], []
+        for k in range(4):
+            level = base + lf // 2 + k + p
+            if isinstance(level, int) and not 2 <= level < 6:
+                continue
+            values.append(tall[f, level, :, 0:count].reshape(2 * count, nc))
+            weights.append((even_weights, odd_weights)[p][k])
+        return taps(weights, values)
+
+    def widen_pair(f, base, lf, count):
+        pair = jnp.concatenate([level_taps(f, base, lf, count), level_taps(f, base, lf + 1, count)], axis=0)
+        return split_dot(pair, widen[...], ((1,), (0,)), 2)
+
+    def refine_speeds():
+        for f in range(3):
+            for lf in (0, 2):
+                out = widen_pair(f, 2 * gz, lf, nr)
+                for k in range(4):
+                    fine[f, lf + k // 2, k % 2] = out[k * nr : (k + 1) * nr]
+
+    def warm_mean(base, l, count):
+        x = widen_pair(3, base, 2 * l, count)
+        x = expansion * x * (1.0 + thermal_expansion_curve * x)
+        return 0.125 * halves(
+            (x[:count] + x[count : 2 * count]) + (x[2 * count : 3 * count] + x[3 * count :])
+        )
+
+    refine_speeds()
     rim_wait(grains, 0)
     lane = lax.broadcasted_iota(jnp.int32, (nr, nc), 1)
 
@@ -412,7 +444,7 @@
         even, uneven = centre[:, :nc], centre[:, nc:]
         left = jnp.concatenate([jnp.where(lane == 0, 0.0, pltpu.roll(uneven, 1, axis=1)), even], axis=1)
         right = jnp.concatenate([uneven, jnp.where(lane == nc - 1, 0.0, pltpu.roll(even, nc - 1, axis=1))], axis=1)
-        w, u, v = [row_taps(lambda s, c: fine[f, lf, s : s + c], OFF, nr, rp) for f in range(3)]
+        w, u, v = [fine[f, lf, rp] for f in range(3)]
         flux = advect(w, centre, lower, upper) + advect(v, centre, before, after) + advect(u, centre, left, right)
         around = (lower + upper) + (before + after) + (left + right)
         return centre, (4.0 * salt_diffusion) * (around - 6.0 * centre) - 2.0 * flux
@@ -430,8 +462,6 @@
     walls(grains_mid)
     rim_start(grains_mid, 1)
 
-    for lf in range(8):
-        warm[lf] = level_taps(cols, 3, 0, lf)
     mean_landed(0).wait_recv()
 
     @pl.when(r > 0)
@@ -445,7 +475,7 @@
         mean_landed(4).wait_recv()
 
     for l in range(4):
-        heat_part = warm_mean(frame, lo, lambda i, s, c: warm[i, s : s + c], l)
+        heat_part = warm_mean(0, l, frame)
         buoy[l] = heat_part - contraction * mean_salt[l, lo : lo + frame]
 
     def coarse_step(buf, level, start, count, lift):
@@ -479,12 +509,11 @@
         for f, (q, rate) in enumerate(coarse_step(fields, level + 1, lo, frame, buoy[level])):
             mids[f, level + 1, lo : lo + frame] = jnp.where(inside, q + time_step * rate, 0.0)
 
-    widen_all(mids, cols_mid)
-    for lf in range(4):
-        warm[lf] = level_taps(cols_mid, 3, 2 * gz, lf)
+    for z in range(2):
+        refine_rows(mids, z, OFF, nr)
     results = []
     for l in range(2):
-        lift = warm_mean(nr, OFF, lambda i, s, c: warm[i, s : s + c], l) - contraction * mean_mid[l]
+        lift = warm_mean(2 * gz, l, nr) - contraction * mean_mid[l]
         level = gz * 2 + l + 1
         steps = coarse_step(mids, level, OFF, nr, lift)
         results.append(
@@ -505,9 +534,7 @@
         ends[-1].start()
     landed[gy] = outgoing[gy]
 
-    for f in range(3):
-        for lf in range(4):
-            fine[f, lf] = level_taps(cols_mid, f, 2 * gz, lf)
+    refine_speeds()
     rim_wait(grains_mid, 1)
     parts = []
     for lf in range(4):
@@ -519,14 +546,24 @@
         for rp in range(2):
             k = (lf * 2 + rp) * nr
             for c in range(nc // 64):
-                salt_out[lf, c, pl.ds(rp, nr, stride=2), :] = whole[k : k + nr, 128 * c : 128 * (c + 1)]
+                salt[lf, c, pl.ds(rp, nr, stride=2), :] = whole[k : k + nr, 128 * c : 128 * (c + 1)]
+
+    stores = [
+        pltpu.make_async_copy(salt.at[:, c], salt_out.at[:, :, 128 * c : 128 * (c + 1)], load.at[2 + c])
+        for c in range(nc // 64)
+    ]
+    for copy in stores:
+        copy.start()
 
     for d in range(1, n):
         j = lax.rem(gy + n - d, n)
         remote(outgoing.at[j], landed.at[j], end_send.at[d], end_recv.at[j], gx, j, gz).wait_recv()
     back = landed[...].reshape(ny, lanes).T
-    vel_out[...] = back[: 6 * cx].reshape(3, 2, cx, ny)
-    heat_out[...] = back[6 * cx :].reshape(2, cx, ny)
+    flow[...] = back[: 6 * cx].reshape(3, 2, cx, ny)
+    heat[...] = back[6 * cx :].reshape(2, cx, ny)
+    stores += [pltpu.make_async_copy(flow, vel_out, load.at[0]), pltpu.make_async_copy(heat, heat_out, load.at[1])]
+    for copy in stores[-2:]:
+        copy.start()
 
     for copy in main + ends:
         copy.wait_send()
@@ -553,6 +590,19 @@
     def _():
         mean_copy(3).wait_send()
         mean_copy(4).wait_send()
+
+    for copy in stores:
+        copy.wait()
+
+
+def store(vel, temp, salt, vel_out, temp_out, salt_out, sems):
+    copies = [pltpu.make_async_copy(vel, vel_out, sems.at[0]), pltpu.make_async_copy(temp, temp_out, sems.at[1])]
+    for lf in range(4):
+        copies.append(pltpu.make_async_copy(salt.at[lf], salt_out.at[lf], sems.at[2 + lf]))
+    for copy in copies:
+        copy.start()
+    for copy in copies:
+        copy.wait()
 
 
 def on_device(ngx, n, flow, heat, salt):
@@ -561,18 +611,20 @@
     padded = nr + 2 * OFF
     lanes = 8 * cx
     f32, dma = jnp.float32, pltpu.SemaphoreType.DMA
-    vmem = pl.BlockSpec(memory_space=pltpu.VMEM)
-    split = salt.reshape(4, 2 * nr, nc // 64, 128).transpose(0, 2, 1, 3)
+    hbm = pl.BlockSpec(memory_space=pltpu.HBM)
     vel, temp, out = pl.pallas_call(
         functools.partial(kernel, ngx, n, nr, nc, cx, ny),
         out_shape=(
             jax.ShapeDtypeStruct(flow.shape, f32),
             jax.ShapeDtypeStruct(heat.shape, f32),
-            jax.ShapeDtypeStruct(split.shape, f32),
+            jax.ShapeDtypeStruct(salt.shape, f32),
         ),
-        in_specs=[vmem] * 3,
-        out_specs=(vmem,) * 3,
+        in_specs=[hbm] * 3,
+        out_specs=(hbm,) * 3,
         scratch_shapes=[
+            pltpu.VMEM(flow.shape, f32),
+            pltpu.VMEM(heat.shape, f32),
+            pltpu.VMEM((4, nc // 64, 2 * nr, 128), f32),
             pltpu.VMEM((ny + 16, lanes), f32),
             pltpu.VMEM((n, nr + 8, lanes), f32),
             pltpu.VMEM((2, 8, lanes), f32),
@@ -580,10 +632,8 @@
             pltpu.VMEM((2, n, 8, lanes), f32),
             pltpu.VMEM((4, 6, padded, nc), f32),
             pltpu.VMEM((4, 6, padded, nc), f32),
-            pltpu.VMEM((4, 8, padded, 2 * nc), f32),
-            pltpu.VMEM((4, 8, padded, 2 * nc), f32),
-            pltpu.VMEM((8, padded, 2 * nc), f32),
-            pltpu.VMEM((3, 4, padded, 2 * nc), f32),
+            pltpu.VMEM((4, 8, 2, nr + 2 * WIDE, nc), f32),
+            pltpu.VMEM((3, 4, 2, nr, 2 * nc), f32),
             pltpu.VMEM((6, 2, padded, 2 * nc), f32),
             pltpu.VMEM((6, 2, padded, 2 * nc), f32),
             pltpu.VMEM((4, padded, nc), f32),
@@ -593,13 +643,20 @@
             pltpu.VMEM((2 * nc, 2 * nc), jnp.bfloat16),
             pltpu.VMEM((nc, 2 * nc), jnp.bfloat16),
             dma((n,)), dma((2, n)), dma((n,)), dma((2, 2)), dma((2, n)), dma((5,)), dma((5,)),
-            dma((2, 3)), dma((2, 3)), dma((n,)), dma((n,)),
+            dma((2, 3)), dma((2, 3)), dma((n,)), dma((n,)), dma((2 + nc // 64,)),
         ],
         compiler_params=pltpu.CompilerParams(
-            collective_id=0, has_side_effects=True, vmem_limit_bytes=48 * 1024 * 1024
+            collective_id=0, has_side_effects=True, vmem_limit_bytes=VMEM
         ),
-    )(flow, heat, split)
-    return vel, temp, out.transpose(0, 2, 1, 3).reshape(salt.shape)
+    )(flow, heat, salt)
+    return pl.pallas_call(
+        store,
+        out_shape=tuple(jax.ShapeDtypeStruct(a.shape, f32) for a in (flow, heat, salt)),
+        in_specs=[hbm] * 3,
+        out_specs=(hbm,) * 3,
+        scratch_shapes=[dma((6,))],
+        compiler_params=pltpu.CompilerParams(vmem_limit_bytes=VMEM),
+    )(vel, temp, out)
 
 
 def solution(mesh):

time: 29.6 us -> 38.2 us (1.29)
  Pallas kernels: 25 us -> 37.4 us
  local copies, waits for them, and re-layouts: 3.8 us -> 0 us
    pallas_call x0 -> x1, Pallas kernels: none -> 13.1 us  [on_device(): pl.pallas_call(store, out_shape=tuple((jax.ShapeDtypeStruct(a.shape, f32)...]
    unnamed x8 -> x0, local copies, waits for them, and re-layouts: 3.05 us -> none
    reshape x1 -> x0, local copies, waits for them, and re-layouts: 0.73 us -> none  [on_device(): return (vel, temp, out.transpose(0, 2, 1, 3).reshape(salt.shape))]
    pallas_call x1, Pallas kernels: 25 us -> 24.3 us  [on_device(): pl.pallas_call(functools.partial(kernel, ngx, n, nr, nc, cx, ny), out_sha...]
where the time goes in v2:
time: 38.2 us; the launch traced here: 38 us
  Pallas kernels  37.4 us (98%)
  between operations  0.64 us (2%)
    pallas_call x1, Pallas kernels, on_device(): pl.pallas_call(functools.partial(kernel, ngx, n, nr, nc, cx, ny), out_sha...  24.3 us
    pallas_call x1, Pallas kernels, on_device(): pl.pallas_call(store, out_shape=tuple((jax.ShapeDtypeStruct(a.shape, f32)...  13.1 us

profile of v2, /device:TPU:0, one launch (start us, length us, event | category | flops | bytes accessed | tf_op | source)
XLA Modules:
  0.0 38.0 jit_solution(15321753615045172634)
XLA Ops:
  0.6 24.3 %shard_map.58 = (f32[3,2,32,128]{3,2,1,0:T(8,128)}, f32[2,32,128]{2,1,0:T(8,128)}, f32[4,32,512]{2,1,0:T(8,128)}) custom-call(f32[3,2,32,128]{3,2,1,0:T(8,128)} %flow_in.1, f32[2,32,128]{2,1,0:T(8,128)} %heat_in.1, f32[4,32,512]{2,1,0:T(8,128)} %salt_in.1), custom_call_target="tpu_custom_call" | custom-call | tf_op jit(solution)/shard_map/pallas_call | solution.py:615
  25.0 13.1 %shard_map.59 = (f32[3,2,32,128]{3,2,1,0:T(8,128)}, f32[2,32,128]{2,1,0:T(8,128)}, f32[4,32,512]{2,1,0:T(8,128)}) custom-call(f32[3,2,32,128]{3,2,1,0:T(8,128)} %get-tuple-element.6.vel, f32[2,32,128]{2,1,0:T(8,128)} %get-tuple-element.7.temp, f32[4,32,512]{2,1,0:T(8,128)} %get-tuple-element.8.salt), custom_call_target="tpu_custom_call" | custom-call | tf_op jit(solution)/shard_map/pallas_call | solution.py:652

commit v3 on v2

--- a/solution.py
+++ b/solution.py
@@ -52,7 +52,7 @@
     ngx, n, nr, nc, cx, ny,
     flow_in, heat_in, salt_in, vel_out, heat_out, salt_out,
     flow, heat, salt, turned, message, edge, got, got_edge, fields, mids, tall, fine,
-    grains, grains_mid, mean_salt, buoy, outgoing, landed, fold, widen,
+    grains, grains_mid, mean_salt, results, outgoing, landed, fold, widen,
     main_send, main_recv, pass_send, edge_send, edge_recv, mean_send, mean_recv,
     rim_send, rim_recv, end_send, end_recv, load,
 ):
@@ -141,11 +141,13 @@
             device_id=at(x, y, z), device_id_type=pl.DeviceIdType.MESH,
         )
 
-    main = []
-    for d in range(1, n):
+    def main(d):
         to = lax.rem(gy + d, n)
-        main.append(remote(message.at[to], got.at[gz, gy], main_send.at[d], main_recv.at[gz, gy], gx, to, gz))
-        main[-1].start()
+        return remote(message.at[to], got.at[gz, gy], main_send.at[d], main_recv.at[gz, gy], gx, to, gz)
+
+    @pl.loop(1, n)
+    def _(d):
+        main(d).start()
 
     def passed(j, z):
         return remote(got.at[z, j], got.at[z, j], pass_send.at[j], main_recv.at[z, j], gx, gy, other)
@@ -318,7 +320,8 @@
         mean_copy(3).start()
         mean_copy(4).start()
 
-    for d in range(1, n):
+    @pl.loop(1, n)
+    def _(d):
         j = lax.rem(gy + n - d, n)
         passed(j, gz).wait_recv()
         passed(j, gz).start()
@@ -358,25 +361,22 @@
         return out
 
     def assemble(z):
-        for t in range(lanes // 128):
-            for a in range(n // per):
-                values = []
-                for j in range(per):
-                    body = got[z, per * a + j, 0:nr, 128 * t : 128 * (t + 1)]
-                    rim = (
-                        got[z, per * a + j, nr : nr + 8, 128 * t : 128 * (t + 1)]
-                        + got_edge[z, per * a + j, :, 128 * t : 128 * (t + 1)]
-                    )
-                    values.append(jnp.concatenate([body, rim], axis=0))
-                for k in range(per):
-                    pair = per * t + k
-                    f, l = pair // 2, pair % 2
-                    whole = gather_chunks(values, k)
-                    where = slice(128 * a, 128 * (a + 1))
-                    level = z * 2 + l + 1
-                    fields[f, level, OFF : OFF + nr, where] = whole[:nr]
-                    fields[f, level, 0:8, where] = whole[nr:]
-                    fields[f, level, OFF + nr : padded, where] = whole[nr:]
+        @pl.loop(0, (lanes // 128) * (n // per))
+        def _(i):
+            t, a = i // (n // per), lax.rem(i, n // per)
+            part = pl.ds(pl.multiple_of(128 * t, 128), 128)
+            where = pl.ds(pl.multiple_of(128 * a, 128), 128)
+            values = []
+            for j in range(per):
+                body = got[z, per * a + j, 0:nr, part]
+                rim = got[z, per * a + j, nr : nr + 8, part] + got_edge[z, per * a + j, :, part]
+                values.append(jnp.concatenate([body, rim], axis=0))
+            for k in range(per):
+                whole = gather_chunks(values, k)
+                f, level = (per // 2) * t + k // 2, z * 2 + k % 2 + 1
+                fields[f, level, OFF : OFF + nr, where] = whole[:nr]
+                fields[f, level, 0:8, where] = whole[nr:]
+                fields[f, level, OFF + nr : padded, where] = whole[nr:]
 
     lo = OFF - WIDE
 
@@ -386,45 +386,44 @@
         return taps(weights, [buf[f, level, base + k : base + k + count] for k in range(4)])
 
     def refine_rows(buf, z, start, count):
-        for l in range(2):
+        @pl.loop(0, 6)
+        def _(i):
+            f, level = i // 2, z * 2 + lax.rem(i, 2)
+            for rp in range(2):
+                tall[f, level + 2, rp, 0:nr] = row_taps(buf, f, level + 1, OFF, nr, rp)
+
+        @pl.loop(0, 2)
+        def _(l):
             level = z * 2 + l
             for rp in range(2):
-                for f in range(3):
-                    tall[f, level + 2, rp, 0:nr] = row_taps(buf, f, level + 1, OFF, nr, rp)
                 tall[3, level + 2, rp, 0:count] = row_taps(buf, 3, level + 1, start, count, rp)
 
     assemble(gz)
     refine_rows(fields, gz, lo, frame)
-    for d in range(n):
-        j = lax.rem(gy + d, n)
-        passed(j, other).wait_recv()
+    @pl.loop(0, n)
+    def _(d):
+        passed(lax.rem(gy + d, n), other).wait_recv()
+
     assemble(other)
     refine_rows(fields, other, lo, frame)
 
-    def level_taps(f, base, lf, count):
-        p = lf % 2
-        values, weights = [], []
-        for k in range(4):
-            level = base + lf // 2 + k + p
-            if isinstance(level, int) and not 2 <= level < 6:
-                continue
-            values.append(tall[f, level, :, 0:count].reshape(2 * count, nc))
-            weights.append((even_weights, odd_weights)[p][k])
-        return taps(weights, values)
-
-    def widen_pair(f, base, lf, count):
-        pair = jnp.concatenate([level_taps(f, base, lf, count), level_taps(f, base, lf + 1, count)], axis=0)
-        return split_dot(pair, widen[...], ((1,), (0,)), 2)
+    def level_taps(f, first, p, count):
+        values = [tall[f, first + k + p, :, 0:count].reshape(2 * count, nc) for k in range(4)]
+        return taps((even_weights, odd_weights)[p], values)
+
+    def widen_pairs(f, firsts, count):
+        parts = [level_taps(f, first, p, count) for first in firsts for p in range(2)]
+        return split_dot(jnp.concatenate(parts, axis=0), widen[...], ((1,), (0,)), 2)
 
     def refine_speeds():
-        for f in range(3):
-            for lf in (0, 2):
-                out = widen_pair(f, 2 * gz, lf, nr)
-                for k in range(4):
-                    fine[f, lf + k // 2, k % 2] = out[k * nr : (k + 1) * nr]
-
-    def warm_mean(base, l, count):
-        x = widen_pair(3, base, 2 * l, count)
+        @pl.loop(0, 3)
+        def _(f):
+            out = widen_pairs(f, (2 * gz, 2 * gz + 1), nr)
+            for k in range(8):
+                fine[f, k // 2, k % 2] = out[k * nr : (k + 1) * nr]
+
+    def warm_mean(level, count):
+        x = widen_pairs(3, (level,), count)
         x = expansion * x * (1.0 + thermal_expansion_curve * x)
         return 0.125 * halves(
             (x[:count] + x[count : 2 * count]) + (x[2 * count : 3 * count] + x[3 * count :])
@@ -449,16 +448,12 @@
         around = (lower + upper) + (before + after) + (left + right)
         return centre, (4.0 * salt_diffusion) * (around - 6.0 * centre) - 2.0 * flux
 
-    mean_mid = []
-    for l in range(2):
-        total = None
-        for lf in (2 * l, 2 * l + 1):
-            for rp in range(2):
-                centre, rate = salt_rate(grains, lf, rp)
-                mid = centre + time_step * rate
-                grains_mid[lf + 1, rp, OFF : OFF + nr] = mid
-                total = mid if total is None else total + mid
-        mean_mid.append(0.125 * halves(total))
+    @pl.loop(0, 4)
+    def _(lf):
+        for rp in range(2):
+            centre, rate = salt_rate(grains, lf, rp)
+            grains_mid[lf + 1, rp, OFF : OFF + nr] = centre + time_step * rate
+
     walls(grains_mid)
     rim_start(grains_mid, 1)
 
@@ -473,10 +468,6 @@
     def _():
         mean_landed(3).wait_recv()
         mean_landed(4).wait_recv()
-
-    for l in range(4):
-        heat_part = warm_mean(0, l, frame)
-        buoy[l] = heat_part - contraction * mean_salt[l, lo : lo + frame]
 
     def coarse_step(buf, level, start, count, lift):
         here = lax.broadcasted_iota(jnp.int32, (count, nc), 1)
@@ -505,42 +496,55 @@
         for level in range(4):
             mids[f, level + 1, 0:8] = jnp.zeros((8, nc), f32)
             mids[f, level + 1, OFF + nr : padded] = jnp.zeros((8, nc), f32)
-    for level in range(4):
-        for f, (q, rate) in enumerate(coarse_step(fields, level + 1, lo, frame, buoy[level])):
+
+    @pl.loop(0, 4)
+    def _(level):
+        lift = warm_mean(level, frame) - contraction * mean_salt[level, lo : lo + frame]
+        for f, (q, rate) in enumerate(coarse_step(fields, level + 1, lo, frame, lift)):
             mids[f, level + 1, lo : lo + frame] = jnp.where(inside, q + time_step * rate, 0.0)
 
     for z in range(2):
         refine_rows(mids, z, OFF, nr)
-    results = []
-    for l in range(2):
-        lift = warm_mean(2 * gz, l, nr) - contraction * mean_mid[l]
-        level = gz * 2 + l + 1
-        steps = coarse_step(mids, level, OFF, nr, lift)
-        results.append(
-            [0.5 * fields[f, level, OFF : OFF + nr] + 0.5 * (q + time_step * rate) for f, (q, rate) in enumerate(steps)]
-        )
-    for a in range(n // per):
-        for t in range(lanes // 128):
-            values = []
-            for k in range(per):
-                pair = per * t + k
-                values.append(results[pair % 2][pair // 2][:, 128 * a : 128 * (a + 1)])
-            for j in range(per):
-                outgoing[per * a + j, :, 128 * t : 128 * (t + 1)] = gather_chunks(values, j)
-    ends = []
-    for d in range(1, n):
+
+    @pl.loop(0, 2)
+    def _(l):
+        salts = sum(grains_mid[1 + 2 * l + p, q, OFF : OFF + nr] for p in range(2) for q in range(2))
+        level = gz * 2 + l
+        lift = warm_mean(level, nr) - (0.125 * contraction) * halves(salts)
+        for f, (q, rate) in enumerate(coarse_step(mids, level + 1, OFF, nr, lift)):
+            results[2 * f + l] = 0.5 * fields[f, level + 1, OFF : OFF + nr] + 0.5 * (q + time_step * rate)
+
+    @pl.loop(0, (lanes // 128) * (n // per))
+    def _(i):
+        t, a = i // (n // per), lax.rem(i, n // per)
+        part = pl.ds(pl.multiple_of(128 * t, 128), 128)
+        where = pl.ds(pl.multiple_of(128 * a, 128), 128)
+        values = [results[per * t + k, :, where] for k in range(per)]
+        for j in range(per):
+            outgoing[per * a + j, :, part] = gather_chunks(values, j)
+
+    def end(d):
         to = lax.rem(gy + d, n)
-        ends.append(remote(outgoing.at[to], landed.at[gy], end_send.at[d], end_recv.at[gy], gx, to, gz))
-        ends[-1].start()
+        return remote(outgoing.at[to], landed.at[gy], end_send.at[d], end_recv.at[gy], gx, to, gz)
+
+    @pl.loop(1, n)
+    def _(d):
+        end(d).start()
+
     landed[gy] = outgoing[gy]
 
     refine_speeds()
     rim_wait(grains_mid, 1)
-    parts = []
-    for lf in range(4):
+
+    @pl.loop(0, 4)
+    def _(lf):
         for rp in range(2):
             centre, rate = salt_rate(grains_mid, lf, rp)
-            parts.append(0.5 * grains[lf + 1, rp, OFF : OFF + nr] + 0.5 * (centre + time_step * rate))
+            grains[lf + 1, rp, OFF : OFF + nr] = 0.5 * grains[lf + 1, rp, OFF : OFF + nr] + 0.5 * (
+                centre + time_step * rate
+            )
+
+    parts = [grains[lf + 1, rp, OFF : OFF + nr] for lf in range(4) for rp in range(2)]
     whole = split_dot(jnp.concatenate(parts, axis=0), fold[...], ((1,), (1,)))
     for lf in range(4):
         for rp in range(2):
@@ -555,9 +559,11 @@
     for copy in stores:
         copy.start()
 
-    for d in range(1, n):
+    @pl.loop(1, n)
+    def _(d):
         j = lax.rem(gy + n - d, n)
         remote(outgoing.at[j], landed.at[j], end_send.at[d], end_recv.at[j], gx, j, gz).wait_recv()
+
     back = landed[...].reshape(ny, lanes).T
     flow[...] = back[: 6 * cx].reshape(3, 2, cx, ny)
     heat[...] = back[6 * cx :].reshape(2, cx, ny)
@@ -565,10 +571,15 @@
     for copy in stores[-2:]:
         copy.start()
 
-    for copy in main + ends:
-        copy.wait_send()
-    for j in range(n):
+    @pl.loop(1, n)
+    def _(d):
+        main(d).wait_send()
+        end(d).wait_send()
+
+    @pl.loop(0, n)
+    def _(j):
         passed(j, gz).wait_send()
+
     mean_copy(0).wait_send()
 
     @pl.when(gx < ngx - 1)
@@ -595,14 +606,25 @@
         copy.wait()
 
 
-def store(vel, temp, salt, vel_out, temp_out, salt_out, sems):
-    copies = [pltpu.make_async_copy(vel, vel_out, sems.at[0]), pltpu.make_async_copy(temp, temp_out, sems.at[1])]
-    for lf in range(4):
-        copies.append(pltpu.make_async_copy(salt.at[lf], salt_out.at[lf], sems.at[2 + lf]))
-    for copy in copies:
-        copy.start()
-    for copy in copies:
-        copy.wait()
+def store(*refs):
+    ins, outs, held, sems = refs[:3], refs[3:6], refs[6:9], refs[9]
+    pairs = []
+    for k in range(3):
+        for i in range(ins[k].shape[0]):
+            sem = sems.at[k, i]
+            pairs.append(
+                (
+                    pltpu.make_async_copy(ins[k].at[i], held[k].at[i], sem),
+                    pltpu.make_async_copy(held[k].at[i], outs[k].at[i], sem),
+                )
+            )
+    for first, _ in pairs:
+        first.start()
+    for first, second in pairs:
+        first.wait()
+        second.start()
+    for _, second in pairs:
+        second.wait()
 
 
 def on_device(ngx, n, flow, heat, salt):
@@ -637,7 +659,7 @@
             pltpu.VMEM((6, 2, padded, 2 * nc), f32),
             pltpu.VMEM((6, 2, padded, 2 * nc), f32),
             pltpu.VMEM((4, padded, nc), f32),
-            pltpu.VMEM((4, nr + 2 * WIDE, nc), f32),
+            pltpu.VMEM((8, nr, nc), f32),
             pltpu.VMEM((n, nr, lanes), f32),
             pltpu.VMEM((n, nr, lanes), f32),
             pltpu.VMEM((2 * nc, 2 * nc), jnp.bfloat16),
@@ -654,7 +676,7 @@
         out_shape=tuple(jax.ShapeDtypeStruct(a.shape, f32) for a in (flow, heat, salt)),
         in_specs=[hbm] * 3,
         out_specs=(hbm,) * 3,
-        scratch_shapes=[dma((6,))],
+        scratch_shapes=[pltpu.VMEM(a.shape, f32) for a in (flow, heat, salt)] + [dma((3, 4))],
         compiler_params=pltpu.CompilerParams(vmem_limit_bytes=VMEM),
     )(vel, temp, out)
 

time: 38.2 us -> 28.4 us (0.74)
  Pallas kernels: 37.4 us -> 27.5 us
    pallas_call x1, Pallas kernels: 13.1 us -> 1.76 us  [on_device(): pl.pallas_call(store, out_shape=tuple((jax.ShapeDtypeStruct(a.shape, f32)...]
    pallas_call x1, Pallas kernels: 24.3 us -> 25.8 us  [on_device(): pl.pallas_call(functools.partial(kernel, ngx, n, nr, nc, cx, ny), out_sha...]
where the time goes in v3:
time: 28.4 us; the launch traced here: 28.2 us
  Pallas kernels  27.5 us (97%)
  between operations  0.64 us (2%)
    pallas_call x1, Pallas kernels, on_device(): pl.pallas_call(functools.partial(kernel, ngx, n, nr, nc, cx, ny), out_sha...  25.8 us
    pallas_call x1, Pallas kernels, on_device(): pl.pallas_call(store, out_shape=tuple((jax.ShapeDtypeStruct(a.shape, f32)...  1.76 us

profile of v3, /device:TPU:0, one launch (start us, length us, event | category | flops | bytes accessed | tf_op | source)
XLA Modules:
  0.0 28.2 jit_solution(14444440116429875045)
XLA Ops:
  0.6 25.8 %shard_map.58 = (f32[3,2,32,128]{3,2,1,0:T(8,128)}, f32[2,32,128]{2,1,0:T(8,128)}, f32[4,32,512]{2,1,0:T(8,128)}) custom-call(f32[3,2,32,128]{3,2,1,0:T(8,128)} %flow_in.1, f32[2,32,128]{2,1,0:T(8,128)} %heat_in.1, f32[4,32,512]{2,1,0:T(8,128)} %salt_in.1), custom_call_target="tpu_custom_call" | custom-call | tf_op jit(solution)/shard_map/pallas_call | solution.py:637
  26.4 1.8 %shard_map.59 = (f32[3,2,32,128]{3,2,1,0:T(8,128)}, f32[2,32,128]{2,1,0:T(8,128)}, f32[4,32,512]{2,1,0:T(8,128)}) custom-call(f32[3,2,32,128]{3,2,1,0:T(8,128)} %get-tuple-element.6.refs_0_, f32[2,32,128]{2,1,0:T(8,128)} %get-tuple-element.7.refs_1_, f32[4,32,512]{2,1,0:T(8,128)} %get-tuple-element.8.refs_2_), custom_call_target="tpu_custom_call" | custom-call | tf_op jit(solution)/shard_map/pallas_call | solution.py:674

commit v4 on v2

--- a/solution.py
+++ b/solution.py
@@ -262,7 +262,6 @@
             up.wait_send()
 
     walls(grains)
-    rim_start(grains, 0)
 
     def halves(value):
         return value[:, :nc] + value[:, nc:]
@@ -322,6 +321,7 @@
         j = lax.rem(gy + n - d, n)
         passed(j, gz).wait_recv()
         passed(j, gz).start()
+    rim_start(grains, 0)
 
     row_id = lax.broadcasted_iota(jnp.int32, (nc, 2 * nc), 0)
     col_id = lax.broadcasted_iota(jnp.int32, (nc, 2 * nc), 1)
@@ -595,14 +595,25 @@
         copy.wait()
 
 
-def store(vel, temp, salt, vel_out, temp_out, salt_out, sems):
-    copies = [pltpu.make_async_copy(vel, vel_out, sems.at[0]), pltpu.make_async_copy(temp, temp_out, sems.at[1])]
-    for lf in range(4):
-        copies.append(pltpu.make_async_copy(salt.at[lf], salt_out.at[lf], sems.at[2 + lf]))
-    for copy in copies:
-        copy.start()
-    for copy in copies:
-        copy.wait()
+def store(*refs):
+    ins, outs, held, sems = refs[:3], refs[3:6], refs[6:9], refs[9]
+    pairs = []
+    for k in range(3):
+        for i in range(ins[k].shape[0]):
+            sem = sems.at[k, i]
+            pairs.append(
+                (
+                    pltpu.make_async_copy(ins[k].at[i], held[k].at[i], sem),
+                    pltpu.make_async_copy(held[k].at[i], outs[k].at[i], sem),
+                )
+            )
+    for first, _ in pairs:
+        first.start()
+    for first, second in pairs:
+        first.wait()
+        second.start()
+    for _, second in pairs:
+        second.wait()
 
 
 def on_device(ngx, n, flow, heat, salt):
@@ -654,7 +665,7 @@
         out_shape=tuple(jax.ShapeDtypeStruct(a.shape, f32) for a in (flow, heat, salt)),
         in_specs=[hbm] * 3,
         out_specs=(hbm,) * 3,
-        scratch_shapes=[dma((6,))],
+        scratch_shapes=[pltpu.VMEM(a.shape, f32) for a in (flow, heat, salt)] + [dma((3, 4))],
         compiler_params=pltpu.CompilerParams(vmem_limit_bytes=VMEM),
     )(vel, temp, out)
 

time: 38.2 us -> 27.5 us (0.72)
  Pallas kernels: 37.4 us -> 26.7 us
    pallas_call x1, Pallas kernels: 13.1 us -> 1.76 us  [on_device(): pl.pallas_call(store, out_shape=tuple((jax.ShapeDtypeStruct(a.shape, f32)...]
    pallas_call x1, Pallas kernels: 24.3 us -> 24.9 us  [on_device(): pl.pallas_call(functools.partial(kernel, ngx, n, nr, nc, cx, ny), out_sha...]
where the time goes in v4:
time: 27.5 us; the launch traced here: 27.3 us
  Pallas kernels  26.7 us (97%)
  between operations  0.64 us (2%)
    pallas_call x1, Pallas kernels, on_device(): pl.pallas_call(functools.partial(kernel, ngx, n, nr, nc, cx, ny), out_sha...  24.9 us
    pallas_call x1, Pallas kernels, on_device(): pl.pallas_call(store, out_shape=tuple((jax.ShapeDtypeStruct(a.shape, f32)...  1.76 us

profile of v4, /device:TPU:0, one launch (start us, length us, event | category | flops | bytes accessed | tf_op | source)
XLA Modules:
  0.0 27.3 jit_solution(1472435497184441106)
XLA Ops:
  0.6 24.9 %shard_map.58 = (f32[3,2,32,128]{3,2,1,0:T(8,128)}, f32[2,32,128]{2,1,0:T(8,128)}, f32[4,32,512]{2,1,0:T(8,128)}) custom-call(f32[3,2,32,128]{3,2,1,0:T(8,128)} %flow_in.1, f32[2,32,128]{2,1,0:T(8,128)} %heat_in.1, f32[4,32,512]{2,1,0:T(8,128)} %salt_in.1), custom_call_target="tpu_custom_call" | custom-call | tf_op jit(solution)/shard_map/pallas_call | solution.py:626
  25.6 1.8 %shard_map.59 = (f32[3,2,32,128]{3,2,1,0:T(8,128)}, f32[2,32,128]{2,1,0:T(8,128)}, f32[4,32,512]{2,1,0:T(8,128)}) custom-call(f32[3,2,32,128]{3,2,1,0:T(8,128)} %get-tuple-element.6.refs_0_, f32[2,32,128]{2,1,0:T(8,128)} %get-tuple-element.7.refs_1_, f32[4,32,512]{2,1,0:T(8,128)} %get-tuple-element.8.refs_2_), custom_call_target="tpu_custom_call" | custom-call | tf_op jit(solution)/shard_map/pallas_call | solution.py:663
